TPU v7x, 128 devices: a whole 4x4x4 slice. The times are simulated.
128 devices in a mesh: chan: 16 (over x, y), hole: 8 (over z, core).
Axes of the slice: x: 4, y: 4, z: 4, core: 2. Of those that a mesh axis runs over, the one named last changes fastest.
Arguments:
- amplitudes: float32 [64, 1024, 1024], P('chan', None, 'hole'), may hold values from -6 to 6
- interaction: float32 [64, 1024, 1024], P('chan'), may hold values from -0.1875 to 0.1875
- sixj_values: float32 [64], replicated, may hold values from -0.75 to 0.75
- sixj_index: int32 [64, 64], replicated, may hold values from 0 to 63
- ph_rows: int32 [64], P('chan'), may hold values from 1 to 1024, as said below
- denominators: float32 [64, 1024, 1024], P('chan', None, 'hole'), may hold values from 1 to 8
Outputs:
- update: float32 [64, 1024, 1024], P('chan', None, 'hole')
Inputs may be any that keep to these rules, and one draw needn't show every extreme that they name: `ph_rows`: at least one channel has all 1024 rows live.
All inputs are finite; a program needn't handle non-finite values.
Results may differ from a plain program's by a relative error of at most 0.00012.
Values sent between devices are 32-bit elements; how exact they have to be, the bound alone decides.
No kernel may reach another device: no remote copies, remote signals or barrier semaphores. Data moves between devices by JAX's collectives and lax.ppermute only.
A program may use at most 128 MiB of HBM per device.

v0:
```python
import jax
import jax.numpy as jnp
from jax import lax
from jax.sharding import PartitionSpec as P


def mix_rows(table, blocks):
    return jnp.einsum("dc,cph->dph", table, blocks, precision=lax.Precision.HIGHEST)


def recouple(blocks, table):
    rows = lax.all_to_all(blocks, "chan", split_axis=1, concat_axis=0, tiled=True)
    return lax.all_to_all(mix_rows(table, rows), "chan", split_axis=0, concat_axis=1, tiled=True)


def per_device(amplitudes, interaction, sixj_values, sixj_index, ph_rows, denominators):
    hp = lax.Precision.HIGHEST
    slots = jnp.arange(sixj_values.shape[0], dtype=jnp.int32)
    weights = jnp.sum(
        jnp.where(
            sixj_index[:, :, None] == slots[None, None, :],
            sixj_values[None, None, :],
            jnp.float32(0.0),
        ),
        axis=2,
    )
    height = amplitudes.shape[1]
    live = (jnp.arange(height, dtype=jnp.int32)[None, :] < ph_rows[:, None]).astype(jnp.float32)[
        :, :, None
    ]
    recoupled = recouple(amplitudes, weights) * live
    linear = jnp.einsum("dpq,dqh->dph", interaction, recoupled, precision=hp)
    columns = amplitudes.shape[2] * lax.axis_size("hole")
    scale = 1.0 / jnp.sqrt(jnp.float32(height * columns))
    whole = lax.all_gather(recoupled, "hole", axis=2, tiled=True)
    inner = jnp.einsum("dph,dpk->dhk", whole, linear, precision=hp)
    quadratic = jnp.einsum("dph,dhk->dpk", whole, inner, precision=hp)
    cycle = (linear + quadratic * scale) * live
    back = recouple(cycle, weights.T)
    return back / denominators


def solution(mesh):
    in_specs = (
        P("chan", None, "hole"),
        P("chan", None, None),
        P(),
        P(),
        P("chan"),
        P("chan", None, "hole"),
    )
    out_specs = P("chan", None, "hole")
    return jax.shard_map(
        per_device, mesh=mesh, in_specs=in_specs, out_specs=out_specs, check_vma=False
    )
```

profile of v0, /device:TPU:1, one launch (start us, length us, event | category | flops | bytes accessed | tf_op | source)
XLA Modules:
  0.0 285.3 jit_solution(12258953784631652205)
XLA Ops:
  6.5 4.3 %copy.48 = f32[4,1024,128]{2,0,1:T(4,128)} copy(f32[4,1024,128]{2,1,0:T(8,128)} %param.6) | data formatting | bytes 4194304 | tf_op args[0]
  10.8 7.7 %all-to-all-start = ((f32[4,1024,128]{2,0,1:T(4,128)}), f32[4,1024,128]{2,0,1:T(4,128)S(1)}, u32[]{:S(2)}, u32[]{:S(2)}) async-start(f32[4,1024,128]{2,0,1:T(4,128)} %copy.48), calls=%async_computation | async-start | bytes 4194304 | tf_op jit(solution)/shard_map/all_to_all | solution.py:12
  18.5 0.0 copy-done.2
  18.5 1.3 select_reduce_fusion
  19.9 26.5 %all-to-all-done = f32[4,1024,128]{2,0,1:T(4,128)S(1)} async-done(((f32[4,1024,128]{2,0,1:T(4,128)}), f32[4,1024,128]{2,0,1:T(4,128)S(1)}, u32[]{:S(2)}, u32[]{:S(2)}) %all-to-all-start) | async-done | bytes 2097184 | tf_op jit(solution)/shard_map/all_to_all | solution.py:12
  46.4 0.6 copy.49
  47.0 1.9 fusion.1
  48.9 2.5 copy.50
  51.5 4.0 %all-to-all-start.1 = ((f32[64,64,128]{2,1,0:T(8,128)}), f32[64,64,128]{2,1,0:T(8,128)S(1)}, u32[]{:S(2)}, u32[]{:S(2)}) async-start(f32[64,64,128]{2,1,0:T(8,128)} %copy.50), calls=%async_computation.1 | async-start | bytes 4194304 | tf_op jit(solution)/shard_map/all_to_all | solution.py:13
  55.5 0.0 all-gather.2.cloned.1.call-start
  55.6 0.0 copy-done.4
  55.6 0.1 fusion.5
  55.7 25.1 %all-to-all-done.1 = f32[64,64,128]{2,1,0:T(8,128)S(1)} async-done(((f32[64,64,128]{2,1,0:T(8,128)}), f32[64,64,128]{2,1,0:T(8,128)S(1)}, u32[]{:S(2)}, u32[]{:S(2)}) %all-to-all-start.1) | async-done | bytes 2097184 | tf_op jit(solution)/shard_map/all_to_all | solution.py:13
  80.7 1.5 copy.51
  82.2 1.9 copy.52
  84.1 1.5 broadcast_multiply_fusion
  85.6 0.0 all-gather.2.cloned.1.call-update
  85.7 21.8 %fusion.6 = f32[4,128,1024]{2,1,0:T(8,128)S(1)} fusion(f32[4,1024,128]{1,2,0:T(8,128)} %broadcast_multiply_fusion, f32[4,1024,1024]{2,1,0:T(8,128)} %param.7), kind=kOutput, calls=%fused_computation.12 | convolution fusion | flops 6442450944 | bytes 20971520 | tf_op jit(solution)/shard_map/dpq,dqh->dph/dot_general | solution.py:32
  107.4 68.7 %all-gather.2.cloned.1.call-done = f32[4,1024,1024]{1,2,0:T(8,128)} async-done(((f32[4,1024,128]{1,2,0:T(8,128)}), f32[4,1024,1024]{1,2,0:T(8,128)}) %all-gather.2.cloned.1.call-update) | async-done | bytes 16777232 | tf_op jit(solution)/shard_map/all_gather | solution.py:35
  176.2 17.8 %fusion.7 = f32[4,1024,128]{2,1,0:T(8,128)S(1)} fusion(f32[4,1024,1024]{1,2,0:T(8,128)} %all-gather.2.cloned.1.call-done, f32[4,128,1024]{2,1,0:T(8,128)S(1)} %fusion.6), kind=kOutput, calls=%fused_computation.13 | convolution fusion | flops 6442450944 | bytes 20971520 | tf_op jit(solution)/shard_map/dph,dpk->dhk/dot_general | solution.py:36
  194.0 0.0 copy-done
  194.0 11.5 %fusion = f32[4,1024,128]{1,2,0:T(8,128)} fusion(f32[4,128,1024]{2,1,0:T(8,128)S(1)} %fusion.6, f32[4,1024,1024]{1,2,0:T(8,128)S(1)} %copy-done, f32[4,1024,128]{2,1,0:T(8,128)S(1)} %fusion.7, f32[4,1024]{1,0:T(4,128)S(1)} %fusion.5), kind=kOutput, calls=%fused_computation.2 | convolution fusion | flops 6444023808 | bytes 23085056 | tf_op jit(solution)/shard_map/dph,dhk->dpk/dot_general | solution.py:37
  205.5 2.0 copy.55
  207.5 33.5 %all_to_all.72 = f32[4,1024,128]{2,0,1:T(4,128)S(1)} all-to-all(f32[4,1024,128]{2,0,1:T(4,128)S(1)} %copy.55), channel_id=1, replica_groups=mesh['chan'=16,'hole'=8] {'chan'}, dimensions={1} | all-to-all | bytes 4194304 | tf_op jit(solution)/shard_map/all_to_all | solution.py:12
  241.0 0.1 copy.56
  241.2 1.4 copy.57
  242.5 1.9 fusion.3
  244.5 1.2 copy.59
  245.7 29.6 %all_to_all.73 = f32[64,64,128]{2,1,0:T(8,128)S(1)} all-to-all(f32[64,64,128]{2,1,0:T(8,128)S(1)} %copy.59), channel_id=1, replica_groups=mesh['chan'=16,'hole'=8] {'chan'}, dimensions={0} | all-to-all | bytes 4194304 | tf_op jit(solution)/shard_map/all_to_all | solution.py:13
  275.2 0.2 copy.60
  275.5 1.3 copy-done.1
  276.8 1.6 bitcast_divide_fusion
  (6 shorter events, 0.0 us)
Async XLA Ops:
  10.8 7.7 %copy-start.2 = (s32[64,64]{1,0:T(8,128)S(1)}, s32[64,64]{1,0:T(8,128)}, u32[]{:S(2)}) copy-start(s32[64,64]{1,0:T(8,128)} %param.9) | copy-start | bytes 49156
  10.8 7.7 %copy-start.3 = (f32[64]{0:T(128)S(1)}, f32[64]{0:T(128)}, u32[]{:S(2)}) copy-start(f32[64]{0:T(128)} %param.8) | copy-start | bytes 772
  10.8 35.6 %all-to-all-start = ((f32[4,1024,128]{2,0,1:T(4,128)}), f32[4,1024,128]{2,0,1:T(4,128)S(1)}, u32[]{:S(2)}, u32[]{:S(2)}) async-start(f32[4,1024,128]{2,0,1:T(4,128)} %copy.48), calls=%async_computation | async-start | bytes 4194304 | tf_op jit(solution)/shard_map/all_to_all | solution.py:12
  51.5 4.1 %copy-start.4 = (s32[4]{0:T(128)S(1)}, s32[4]{0:T(128)}, u32[]{:S(2)}) copy-start(s32[4]{0:T(128)} %param.10) | copy-start | bytes 52
  51.5 29.2 %all-to-all-start.1 = ((f32[64,64,128]{2,1,0:T(8,128)}), f32[64,64,128]{2,1,0:T(8,128)S(1)}, u32[]{:S(2)}, u32[]{:S(2)}) async-start(f32[64,64,128]{2,1,0:T(8,128)} %copy.50), calls=%async_computation.1 | async-start | bytes 4194304 | tf_op jit(solution)/shard_map/all_to_all | solution.py:13
  55.5 120.6 %all-gather.2.cloned.1.call-start = ((), (), s32[]{:S(2)}) async-start(), calls=%async_computation.4 | async-start | bytes 18874368 | tf_op jit(solution)/shard_map/all_gather | solution.py:35
  176.2 17.8 %copy-start = (f32[4,1024,1024]{1,2,0:T(8,128)S(1)}, f32[4,1024,1024]{1,2,0:T(8,128)}, u32[]{:S(2)}) copy-start(f32[4,1024,1024]{1,2,0:T(8,128)} %all-gather.2.cloned.1.call-done) | copy-start | bytes 50331652
  275.2 1.6 copy-start.1
Sparse Core Ops, SparseCore 0:
  85.8 90.3 all-gather.1
where the time goes:
time: 288 us; the launch traced here: 285 us
  waiting for transfers between devices  120 us (42%)
  blocking collectives  63.1 us (22%)
  matrix products  54.9 us (19%)
  local copies, waits for them, and re-layouts  17.1 us (6%)
  between operations  13.5 us (5%)
  starting transfers between devices  11.8 us (4%)
  other arithmetic  4.49 us (2%)
    all_gather x1, waiting for transfers between devices, per_device(): whole = lax.all_gather(recoupled, 'hole', axis=2, tiled=True)  68.7 us
    all_to_all x1, blocking collectives, recouple(): lax.all_to_all(blocks, 'chan', split_axis=1, concat_axis=0, tiled=True)  33.5 us
    all_to_all x1, blocking collectives, recouple(): lax.all_to_all(mix_rows(table, rows), 'chan', split_axis=0, concat_axis=1...  29.6 us
    all_to_all x1, waiting for transfers between devices, recouple(): lax.all_to_all(blocks, 'chan', split_axis=1, concat_axis=0, tiled=True)  26.5 us
    all_to_all x1, waiting for transfers between devices, recouple(): lax.all_to_all(mix_rows(table, rows), 'chan', split_axis=0, concat_axis=1...  25.1 us
    dot_general x1, matrix products, per_device(): linear = jnp.einsum('dpq,dqh->dph', interaction, recoupled, precision=hp)  21.8 us
    dot_general x1, matrix products, per_device(): inner = jnp.einsum('dph,dpk->dhk', whole, linear, precision=hp)  17.8 us
    dot_general x1, matrix products, per_device(): quadratic = jnp.einsum('dph,dhk->dpk', whole, inner, precision=hp)  11.5 us
  transfers between devices with their start and end apart: 3, of which 3 were waited for; matrix products, arithmetic and copies ran while one was open for 8% of the time, Pallas kernels for 0%

commit v1 on v0

v1 whole, which is shorter than its diff:
```python
import jax
import jax.numpy as jnp
from jax import lax
from jax.sharding import Mesh, PartitionSpec as P

CHIPS = ("chan", "z")


def mix_rows(table, blocks):
    return jnp.einsum("dc,cph->dph", table, blocks, precision=lax.Precision.HIGH)


def per_device(amplitudes, interaction, sixj_values, sixj_index, ph_rows, denominators):
    hp = lax.Precision.HIGH
    slots = jnp.arange(sixj_values.shape[0], dtype=jnp.int32)
    weights = jnp.sum(
        jnp.where(
            sixj_index[:, :, None] == slots[None, None, :],
            sixj_values[None, None, :],
            jnp.float32(0.0),
        ),
        axis=2,
    )
    z = lax.axis_index("z")
    n_chan, n_z = lax.axis_size("chan"), lax.axis_size("z")
    height, width = amplitudes.shape[1:]
    part = height // n_chan
    rows_of = lax.dynamic_index_in_dim(ph_rows, z, 0, keepdims=False)
    live = (jnp.arange(height, dtype=jnp.int32) < rows_of).astype(jnp.float32)[:, None]
    block = lax.dynamic_index_in_dim(interaction, z, 0, keepdims=False)

    rows = lax.all_to_all(amplitudes, "chan", split_axis=1, concat_axis=0, tiled=True)
    mixed = mix_rows(weights, rows)
    mine = lax.all_to_all(mixed, CHIPS, split_axis=0, concat_axis=0, tiled=True)
    mine = mine.reshape(n_chan, n_z, part, width).transpose(0, 2, 1, 3).reshape(height, n_z * width)
    mine = mine * live
    other = lax.ppermute(mine, "core", [(0, 1), (1, 0)])
    linear = jnp.dot(block, mine, precision=hp)
    scale = 1.0 / jnp.sqrt(jnp.float32(height * n_z * width * 2))

    def term(side):
        inner = lax.dot_general(side, linear, (((0,), (0,)), ((), ())), precision=hp)
        return jnp.dot(side, inner, precision=hp)

    cycle = (linear + (term(mine) + term(other)) * scale) * live
    cycle = cycle.reshape(n_chan, part, n_z, width).transpose(0, 2, 1, 3).reshape(-1, part, width)
    spread = lax.all_to_all(cycle, CHIPS, split_axis=0, concat_axis=0, tiled=True)
    back = mix_rows(weights.T, spread)
    back = lax.all_to_all(back, "chan", split_axis=0, concat_axis=1, tiled=True)
    return back / denominators


def solution(mesh):
    split = Mesh(mesh.devices.reshape(mesh.devices.shape[0], -1, 2), ("chan", "z", "core"))
    hole = ("z", "core")
    in_specs = (
        P("chan", None, hole),
        P("chan", None, None),
        P(),
        P(),
        P("chan"),
        P("chan", None, hole),
    )
    return jax.shard_map(
        per_device, mesh=split, in_specs=in_specs, out_specs=P("chan", None, hole), check_vma=False
    )
```

time: 288 us -> 179 us (0.62)
  waiting for transfers between devices: 120 us -> 50.4 us
  matrix products: 54.9 us -> 17.7 us
  between operations: 13.5 us -> 0.19 us
  starting transfers between devices: 11.8 us -> 21.8 us
    all_gather x1 -> x0, waiting for transfers between devices: 68.7 us -> none  [per_device(): whole = lax.all_gather(recoupled, 'hole', axis=2, tiled=True)]
    dot_general x5 -> x7, matrix products: 54.9 us -> 17.7 us  [the longest x1 5.43 us: per_device(): linear = jnp.dot(block, mine, precision=hp)]
    ppermute x0 -> x1, starting transfers between devices: none -> 5.66 us  [per_device(): other = lax.ppermute(mine, 'core', [(0, 1), (1, 0)])]
    all_to_all x6 -> x2, local copies, waits for them, and re-layouts: 5.68 us -> 0.82 us  [the longest x1 0.58 us: per_device(): lax.all_to_all(amplitudes, 'chan', split_axis=1, concat_axis=0, tiled=True)]
    all_to_all x2, starting transfers between devices: 11.8 us -> 16.1 us  [the longest x1 8.42 us: per_device(): mine = lax.all_to_all(mixed, CHIPS, split_axis=0, concat_axis=0, tiled=True)]
    reshape x0 -> x2, local copies, waits for them, and re-layouts: none -> 3.33 us  [the longest x1 1.93 us: per_device(): cycle.reshape(n_chan, part, n_z, width).transpose(0, 2, 1, 3)]
  transfers between devices with their start and end apart: 3 -> 3, of which waited for: 3 -> 2; matrix products, arithmetic and copies ran while one was open for 8% -> 9% of each run, Pallas kernels for 0% -> 0%
where the time goes in v1:
time: 179 us; the launch traced here: 176 us
  blocking collectives  64.5 us (36%)
  waiting for transfers between devices  50.4 us (28%)
  starting transfers between devices  21.8 us (12%)
  matrix products  17.7 us (10%)
  local copies, waits for them, and re-layouts  14.5 us (8%)
  other arithmetic  6.94 us (4%)
    all_to_all x1, blocking collectives, per_device(): lax.all_to_all(cycle, CHIPS, split_axis=0, concat_axis=0, tiled=True)  34.1 us
    all_to_all x1, blocking collectives, per_device(): back = lax.all_to_all(back, 'chan', split_axis=0, concat_axis=1, tiled=True)  30.5 us
    all_to_all x1, waiting for transfers between devices, per_device(): lax.all_to_all(amplitudes, 'chan', split_axis=1, concat_axis=0, tiled=True)  26.5 us
    all_to_all x1, waiting for transfers between devices, per_device(): mine = lax.all_to_all(mixed, CHIPS, split_axis=0, concat_axis=0, tiled=True)  23.8 us
    all_to_all x1, starting transfers between devices, per_device(): mine = lax.all_to_all(mixed, CHIPS, split_axis=0, concat_axis=0, tiled=True)  8.42 us
    all_to_all x1, starting transfers between devices, per_device(): lax.all_to_all(amplitudes, 'chan', split_axis=1, concat_axis=0, tiled=True)  7.72 us
    ppermute x1, starting transfers between devices, per_device(): other = lax.ppermute(mine, 'core', [(0, 1), (1, 0)])  5.66 us
    unnamed x9, local copies, waits for them, and re-layouts  5.62 us
  transfers between devices with their start and end apart: 3, of which 2 were waited for; matrix products, arithmetic and copies ran while one was open for 9% of the time, Pallas kernels for 0%

profile of v1, /device:TPU:1, one launch (start us, length us, event | category | flops | bytes accessed | tf_op | source)
XLA Modules:
  0.0 176.0 jit_solution(11299068322625036360)
XLA Ops:
  0.0 4.3 %copy.26 = f32[4,1024,128]{2,0,1:T(4,128)} copy(f32[4,1024,128]{2,1,0:T(8,128)} %param.6) | data formatting | bytes 4194304 | tf_op args[0]
  4.3 7.7 %all-to-all-start = ((f32[4,1024,128]{2,0,1:T(4,128)}), f32[4,1024,128]{2,0,1:T(4,128)S(1)}, u32[]{:S(2)}, u32[]{:S(2)}) async-start(f32[4,1024,128]{2,0,1:T(4,128)} %copy.26), calls=%async_computation | async-start | bytes 4194304 | tf_op jit(solution)/shard_map/all_to_all | solution.py:32
  12.0 0.0 copy-done.1
  12.0 1.3 select_reduce_fusion
  13.3 26.5 %all-to-all-done = f32[4,1024,128]{2,0,1:T(4,128)S(1)} async-done(((f32[4,1024,128]{2,0,1:T(4,128)}), f32[4,1024,128]{2,0,1:T(4,128)S(1)}, u32[]{:S(2)}, u32[]{:S(2)}) %all-to-all-start) | async-done | bytes 2097184 | tf_op jit(solution)/shard_map/all_to_all | solution.py:32
  39.9 0.6 copy.27
  40.5 1.0 fusion.7
  41.5 2.5 %copy.28 = f32[64,64,128]{2,1,0:T(8,128)} copy(f32[64,64,128]{2,0,1:T(8,128)S(1)} %fusion.7) | data formatting | bytes 4194304 | tf_op jit(solution)/shard_map/dc,cph->dph/dot_general | solution.py:10
  44.0 8.4 %all-to-all-start.1 = ((f32[64,64,128]{2,1,0:T(8,128)}), f32[64,64,128]{2,1,0:T(8,128)S(1)}, u32[]{:S(2)}, u32[]{:S(2)}) async-start(f32[64,64,128]{2,1,0:T(8,128)} %copy.28), calls=%async_computation.1 | async-start | bytes 4194304 | tf_op jit(solution)/shard_map/all_to_all | solution.py:34
  52.5 0.7 dynamic_slice.9
  53.1 0.7 fusion.11
  53.8 23.8 %all-to-all-done.1 = f32[64,64,128]{2,1,0:T(8,128)S(1)} async-done(((f32[64,64,128]{2,1,0:T(8,128)}), f32[64,64,128]{2,1,0:T(8,128)S(1)}, u32[]{:S(2)}, u32[]{:S(2)}) %all-to-all-start.1) | async-done | bytes 2097184 | tf_op jit(solution)/shard_map/all_to_all | solution.py:34
  77.7 1.4 copy.29
  79.1 0.2 bitcast_multiply_fusion
  79.3 5.7 %collective-permute-start = (f32[1024,512]{1,0:T(8,128)S(1)}, f32[1024,512]{1,0:T(8,128)S(1)}, u32[]{:S(2)}, u32[]{:S(2)}) collective-permute-start(f32[1024,512]{1,0:T(8,128)S(1)} %bitcast_multiply_fusion), channel_id=1, source_target_pairs={{0,1},{1,0},{2,3},{3,2},{4,5},{5,4},{6,7},{7,6},{8,9},{9,8},{10,11... | collective-permute-start | bytes 6291464 | tf_op jit(solution)/shard_map/ppermute | solution.py:37
  85.0 0.7 fusion.10
  85.7 2.5 %bitcast_multiply_fusion.1 = f32[16,64,4,128]{3,2,1,0:T(4,128)S(1)} fusion(f32[16,64]{1,0:T(8,128)S(1)} %fusion.10, f32[16,4,64,128]{3,2,1,0:T(8,128)S(1)} %bitcast.43), kind=kLoop, calls=%fused_computation.7 | loop fusion | flops 524288 | bytes 4198400 | tf_op jit(solution)/shard_map/mul | solution.py:36
  88.1 5.4 %fusion = f32[1024,512]{1,0:T(8,128)S(1)} fusion(f32[4,1024,1024]{2,1,0:T(8,128)} %param.7, s32[]{:T(128)S(6)} %select_n.11, f32[128,8,4,128]{3,2,1,0:T(4,128)S(1)} %bitcast.50), kind=kOutput, calls=%fused_computation | convolution fusion | flops 3221225472 | bytes 8388612 | tf_op jit(solution)/shard_map/dot_general | solution.py:38
  93.6 1.9 %fusion.13 = f32[512,512]{1,0:T(8,128)S(1)} fusion(f32[1024,512]{1,0:T(8,128)S(1)} %bitcast_multiply_fusion, f32[1024,512]{1,0:T(8,128)S(1)} %fusion), kind=kOutput, calls=%fused_computation.21 | convolution fusion | flops 1610612736 | bytes 5242880 | tf_op jit(solution)/shard_map/dot_general | solution.py:42
  95.5 1.9 %fusion.14 = f32[1024,512]{1,0:T(8,128)S(1)} fusion(f32[1024,512]{1,0:T(8,128)S(1)} %bitcast_multiply_fusion, f32[512,512]{1,0:T(8,128)S(1)} %fusion.13), kind=kOutput, calls=%fused_computation.22 | convolution fusion | flops 1610612736 | bytes 5242880 | tf_op jit(solution)/shard_map/dot_general | solution.py:43
  97.3 0.0 collective-permute-done
  97.4 1.9 %fusion.15 = f32[512,512]{1,0:T(8,128)S(1)} fusion(f32[1024,512]{1,0:T(8,128)S(1)} %collective-permute-done, f32[1024,512]{1,0:T(8,128)S(1)} %fusion), kind=kOutput, calls=%fused_computation.23 | convolution fusion | flops 1610612736 | bytes 5242880 | tf_op jit(solution)/shard_map/dot_general | solution.py:42
  99.3 3.4 %add_multiply_fusion = f32[1024,512]{1,0:T(8,128)} fusion(f32[1024,512]{1,0:T(8,128)S(1)} %fusion, f32[1024,512]{1,0:T(8,128)S(1)} %fusion.14, f32[1024,512]{1,0:T(8,128)S(1)} %collective-permute-done, f32[512,512]{1,0:T(8,128)S(1)} %fusion.15, f32[1024]{0:T(1024)S(1)} %fusion.11), kind=kOutput, calls=%fused_computation.10 | convolution fusion | flops 1612709888 | bytes 9441280 | tf_op jit(solution)/shard_map/dot_general | solution.py:43
  102.7 1.9 %reshape.28 = f32[16,64,4,128]{3,2,1,0:T(4,128)S(1)} reshape(f32[1024,512]{1,0:T(8,128)} %add_multiply_fusion) | data formatting | bytes 4194304 | tf_op jit(solution)/shard_map/reshape | solution.py:46
  104.6 0.3 copy.30
  104.9 34.1 %all_to_all.46 = f32[64,64,128]{2,1,0:T(8,128)S(1)} all-to-all(f32[64,64,128]{2,1,0:T(8,128)S(1)} %bitcast.48), channel_id=1, replica_groups=mesh['chan'=16,'z'=4,'core'=2] {'chan','z'}, dimensions={0} | all-to-all | bytes 4194304 | tf_op jit(solution)/shard_map/all_to_all | solution.py:47
  139.0 2.2 %fusion.5 = f32[64,64,128]{2,0,1:T(8,128)S(1)} fusion(f32[64,64,128]{2,1,0:T(8,128)S(1)} %all_to_all.46, f32[64,64]{1,0:T(8,128)S(1)} %select_reduce_fusion), kind=kOutput, calls=%fused_computation.8 | convolution fusion | flops 201326592 | bytes 4210688 | tf_op jit(solution)/shard_map/dc,cph->dph/dot_general | solution.py:10
  141.1 1.2 copy.33
  142.4 30.5 %all_to_all.47 = f32[64,64,128]{2,1,0:T(8,128)S(1)} all-to-all(f32[64,64,128]{2,1,0:T(8,128)S(1)} %copy.33), channel_id=1, replica_groups=mesh['chan'=16,'z'=4,'core'=2] {'chan'}, dimensions={0} | all-to-all | bytes 4194304 | tf_op jit(solution)/shard_map/all_to_all | solution.py:49
  172.8 0.2 copy.34
  173.1 1.3 copy-done
  174.4 1.6 bitcast_divide_fusion
  (6 shorter events, 0.0 us)
Async XLA Ops:
  4.3 7.7 %copy-start.1 = (s32[64,64]{1,0:T(8,128)S(1)}, s32[64,64]{1,0:T(8,128)}, u32[]{:S(2)}) copy-start(s32[64,64]{1,0:T(8,128)} %param.9) | copy-start | bytes 49156
  4.3 7.7 %copy-start.2 = (f32[64]{0:T(128)S(1)}, f32[64]{0:T(128)}, u32[]{:S(2)}) copy-start(f32[64]{0:T(128)} %param.8) | copy-start | bytes 772
  4.3 35.6 %all-to-all-start = ((f32[4,1024,128]{2,0,1:T(4,128)}), f32[4,1024,128]{2,0,1:T(4,128)S(1)}, u32[]{:S(2)}, u32[]{:S(2)}) async-start(f32[4,1024,128]{2,0,1:T(4,128)} %copy.26), calls=%async_computation | async-start | bytes 4194304 | tf_op jit(solution)/shard_map/all_to_all | solution.py:32
  44.0 8.4 %copy-start.3 = (s32[4]{0:T(128)S(1)}, s32[4]{0:T(128)}, u32[]{:S(2)}) copy-start(s32[4]{0:T(128)} %param.10) | copy-start | bytes 52
  44.0 33.7 %all-to-all-start.1 = ((f32[64,64,128]{2,1,0:T(8,128)}), f32[64,64,128]{2,1,0:T(8,128)S(1)}, u32[]{:S(2)}, u32[]{:S(2)}) async-start(f32[64,64,128]{2,1,0:T(8,128)} %copy.28), calls=%async_computation.1 | async-start | bytes 4194304 | tf_op jit(solution)/shard_map/all_to_all | solution.py:34
  79.3 18.0 %collective-permute-start = (f32[1024,512]{1,0:T(8,128)S(1)}, f32[1024,512]{1,0:T(8,128)S(1)}, u32[]{:S(2)}, u32[]{:S(2)}) collective-permute-start(f32[1024,512]{1,0:T(8,128)S(1)} %bitcast_multiply_fusion), channel_id=1, source_target_pairs={{0,1},{1,0},{2,3},{3,2},{4,5},{5,4},{6,7},{7,6},{8,9},{9,8},{10,11... | collective-permute-start | bytes 6291464 | tf_op jit(solution)/shard_map/ppermute | solution.py:37
  172.8 1.6 copy-start

commit v2 on v1

v2 whole, which is shorter than its diff:
```python
import functools
import jax
import jax.numpy as jnp
from jax import lax
from jax.experimental import pallas as pl
from jax.experimental.pallas import tpu as pltpu
from jax.sharding import Mesh, PartitionSpec as P

CHIPS = ("chan", "z")
WHOLE, SPLIT = (0, 64), (0, 8, 64)
MIB = 2**20
BF16, F32 = jnp.bfloat16, jnp.float32
ANY = pl.BlockSpec(memory_space=pl.ANY)
FULL = pl.BlockSpec(memory_space=pltpu.VMEM)
SCALAR = pl.BlockSpec(memory_space=pltpu.SMEM)
SUB = 8


def halves(x):
    high = x.astype(BF16)
    return high, (x - high.astype(F32)).astype(BF16)


def dot3(a, b, dims=((1,), (0,))):
    def one(x, y):
        return lax.dot_general(x, y, (dims, ((), ())), preferred_element_type=F32)

    return one(a[0], b[0]) + (one(a[0], b[1]) + one(a[1], b[0]))


def params(mib):
    return pltpu.CompilerParams(vmem_limit_bytes=mib * MIB)


def deal_kernel(cuts, blocks, *outs):
    for c in range(blocks.shape[0]):
        for k, out in enumerate(outs):
            out[:, c] = blocks[c, :, cuts[k] : cuts[k + 1]]


def deal(blocks, n, cuts, step=4):
    c, height, width = blocks.shape
    part = height // n
    sizes = [b - a for a, b in zip(cuts[:-1], cuts[1:])]
    pieces = pl.pallas_call(
        functools.partial(deal_kernel, cuts),
        grid=(n // step,),
        out_shape=[jax.ShapeDtypeStruct((n, c, rows, width), F32) for rows in sizes],
        in_specs=[pl.BlockSpec((c, step, part, width), lambda i: (0, i, 0, 0))],
        out_specs=[pl.BlockSpec((step, c, rows, width), lambda i: (i, 0, 0, 0)) for rows in sizes],
        compiler_params=params(8),
        cost_estimate=pl.CostEstimate(flops=0, bytes_accessed=8 * c * height * width, transcendentals=0),
    )(blocks.reshape(c, n, part, width))
    return [piece.reshape(n * c, rows, width) for piece, rows in zip(pieces, sizes)]


def spread_table(table):
    n = table.shape[0]
    wide = n * SUB
    rows = (lax.broadcasted_iota(jnp.int32, (wide, n), 0) // SUB == lax.broadcasted_iota(jnp.int32, (wide, n), 1)).astype(BF16)
    columns = (lax.broadcasted_iota(jnp.int32, (n, wide), 1) // SUB == lax.broadcasted_iota(jnp.int32, (n, wide), 0)).astype(BF16)
    same = lax.broadcasted_iota(jnp.int32, (wide, wide), 0) % SUB == lax.broadcasted_iota(jnp.int32, (wide, wide), 1) % SUB
    spread = []
    for part in halves(table):
        tall = jnp.dot(rows, part, preferred_element_type=F32).astype(BF16)
        both = jnp.dot(tall, columns, preferred_element_type=F32)
        spread.append(jnp.where(same, both, 0.0).astype(BF16))
    return tuple(spread)


def mix_kernel(table, *refs):
    ins, out = refs[:-1], refs[-1]
    n, _, width = out.shape
    spread = spread_table(table[...])
    groups = [(ref, row) for ref in ins for row in range(0, ref.shape[1], SUB)]
    for at in range(0, len(groups), 2):
        x = jnp.concatenate(
            [ref[:, row : row + SUB, :].reshape(n * SUB, width) for ref, row in groups[at : at + 2]], axis=1
        )
        y = dot3(spread, halves(x))
        for k in range(2):
            out[:, (at + k) * SUB : (at + k + 1) * SUB, :] = y[:, k * width : (k + 1) * width].reshape(n, SUB, width)


def mix(table, pieces):
    n, _, width = pieces[0].shape
    part = sum(p.shape[1] for p in pieces)
    return pl.pallas_call(
        mix_kernel,
        out_shape=jax.ShapeDtypeStruct((n, part, width), F32),
        in_specs=[FULL] * (1 + len(pieces)),
        out_specs=FULL,
        compiler_params=params(16),
        cost_estimate=pl.CostEstimate(
            flops=6 * n * n * part * width * SUB, bytes_accessed=8 * n * part * width, transcendentals=0
        ),
    )(table, *pieces)


def gather_side(ref, rows_of, scratch_high, scratch_low):
    n, part, width = ref.shape
    n_z = scratch_high.shape[1] // width
    for g in range(n // n_z):
        span = slice(g * part, (g + 1) * part)
        live = g * part + lax.broadcasted_iota(jnp.int32, (part, width), 0) < rows_of
        for k in range(n_z):
            high, low = halves(jnp.where(live, ref[g * n_z + k], 0.0))
            scratch_high[span, k * width : (k + 1) * width] = high
            scratch_low[span, k * width : (k + 1) * width] = low


def own_kernel(scale, block, at, rows, side, inter, acc, lin_h, lin_l, v, side_h, side_l, sem):
    height = v.shape[0]
    copies = [
        pltpu.make_async_copy(inter.at[at[0], pl.ds(r, block)], v.at[pl.ds(r, block)], sem.at[r // block])
        for r in range(0, height, block)
    ]
    for copy in copies:
        copy.start()
    gather_side(side, rows[0], side_h, side_l)
    mine = (side_h[...], side_l[...])
    for r, copy in zip(range(0, height, block), copies):
        copy.wait()
        linear = dot3(halves(v[r : r + block]), mine)
        acc[r : r + block] = linear
        lin_h[r : r + block], lin_l[r : r + block] = halves(linear)
    inner = halves(dot3(mine, (lin_h[...], lin_l[...]), ((0,), (0,))) * scale)
    for r in range(0, height, block):
        acc[r : r + block] += dot3(tuple(s[r : r + block] for s in mine), inner)


def own(at, rows, side, inter, scale, block=256):
    n, part, width = side.shape
    height = inter.shape[1]
    cols = n * part * width // height
    sds = jax.ShapeDtypeStruct
    return pl.pallas_call(
        functools.partial(own_kernel, scale, block),
        out_shape=[sds((height, cols), F32), sds((height, cols), BF16), sds((height, cols), BF16)],
        in_specs=[SCALAR, SCALAR, FULL, ANY],
        out_specs=[FULL] * 3,
        scratch_shapes=[
            pltpu.VMEM((height, height), F32),
            pltpu.VMEM((height, cols), BF16),
            pltpu.VMEM((height, cols), BF16),
            pltpu.SemaphoreType.DMA((height // block,)),
        ],
        compiler_params=params(30),
        cost_estimate=pl.CostEstimate(
            flops=12 * height * height * cols, bytes_accessed=4 * height * (height + 3 * cols), transcendentals=0
        ),
    )(at, rows, side, inter)


def other_kernel(scale, cuts, rows, side, base, lin_h, lin_l, *refs):
    outs, (side_h, side_l) = refs[:-2], refs[-2:]
    n, part, width = side.shape
    n_z = side_h.shape[1] // width
    gather_side(side, rows[0], side_h, side_l)
    theirs = (side_h[...], side_l[...])
    inner = halves(dot3(theirs, (lin_h[...], lin_l[...]), ((0,), (0,))) * scale)
    step = 4
    for g0 in range(0, n // n_z, step):
        span = slice(g0 * part, (g0 + step) * part)
        total = base[span] + dot3(tuple(s[span] for s in theirs), inner)
        live = g0 * part + lax.broadcasted_iota(jnp.int32, total.shape, 0) < rows[0]
        total = jnp.where(live, total, 0.0)
        for g in range(step):
            for k in range(n_z):
                tile = total[g * part : (g + 1) * part, k * width : (k + 1) * width]
                for i, out in enumerate(outs):
                    out[(g0 + g) * n_z + k] = tile[cuts[i] : cuts[i + 1]]


def other(rows, side, base, lin_h, lin_l, scale, cuts):
    n, part, width = side.shape
    height, cols = base.shape
    return pl.pallas_call(
        functools.partial(other_kernel, scale, cuts),
        out_shape=[jax.ShapeDtypeStruct((n, b - a, width), F32) for a, b in zip(cuts[:-1], cuts[1:])],
        in_specs=[SCALAR] + [FULL] * 4,
        out_specs=[FULL] * (len(cuts) - 1),
        scratch_shapes=[pltpu.VMEM((height, cols), BF16)] * 2,
        compiler_params=params(24),
        cost_estimate=pl.CostEstimate(
            flops=12 * height * cols * cols, bytes_accessed=16 * height * cols, transcendentals=0
        ),
    )(rows, side, base, lin_h, lin_l)


def exchange(pieces, axes):
    return [lax.all_to_all(piece, axes, split_axis=0, concat_axis=0, tiled=True) for piece in pieces]


def weights_of(values, index):
    slots = jnp.arange(values.shape[0], dtype=jnp.int32)
    return jnp.sum(jnp.where(index[:, :, None] == slots[None, None, :], values[None, None, :], jnp.float32(0.0)), axis=2)


def per_device(amplitudes, interaction, sixj_values, sixj_index, ph_rows, denominators):
    c, height, width = amplitudes.shape
    n_chan, n_z = lax.axis_size("chan"), lax.axis_size("z")
    z, core = lax.axis_index("z"), lax.axis_index("core")
    at = jnp.reshape(z, (1,)).astype(jnp.int32)
    rows_of = lax.dynamic_slice_in_dim(ph_rows, z, 1)
    scale = 1.0 / (height * width * n_z * 2) ** 0.5

    def forward(cuts):
        def run(blocks, values, index):
            weights = weights_of(values, index)
            mixed = mix(weights, exchange(deal(blocks, n_chan, cuts), "chan"))
            return exchange([mixed], CHIPS)[0], weights

        return run

    def backward(cuts):
        def run(rows, theirs, base, lin_h, lin_l, weights, below):
            cycle = other(rows, theirs, base, lin_h, lin_l, scale, cuts)
            back = mix(weights.T, exchange(cycle, CHIPS))
            back = exchange([back], "chan")[0]
            back = back.reshape(n_chan, c, height // n_chan, width).transpose(1, 0, 2, 3).reshape(c, height, width)
            return back / below

        return run

    mine, weights = lax.cond(core == 0, forward(WHOLE), forward(SPLIT), amplitudes, sixj_values, sixj_index)
    theirs = lax.ppermute(mine, "core", [(0, 1), (1, 0)])
    base, lin_h, lin_l = own(at, rows_of, mine, interaction, scale)
    return lax.cond(
        core == 0, backward(WHOLE), backward(SPLIT), rows_of, theirs, base, lin_h, lin_l, weights, denominators
    )


def solution(mesh):
    split = Mesh(mesh.devices.reshape(mesh.devices.shape[0], -1, 2), ("chan", "z", "core"))
    hole = ("z", "core")
    in_specs = (
        P("chan", None, hole),
        P("chan", None, None),
        P(),
        P(),
        P("chan"),
        P("chan", None, hole),
    )
    return jax.shard_map(
        per_device, mesh=split, in_specs=in_specs, out_specs=P("chan", None, hole), check_vma=False
    )
```

time: 179 us -> 165 us (0.922); the launches traced: 176 us -> 165 us
  Pallas kernels: 0 us -> 22.5 us
  blocking collectives: 64.5 us -> 85.8 us
  matrix products: 17.7 us -> 0 us
  waiting for transfers between devices: 50.4 us -> 32.8 us
  starting transfers between devices: 21.8 us -> 8.4 us
  other arithmetic: 6.94 us -> 2.2 us
  local copies, waits for them, and re-layouts: 14.5 us -> 12.6 us
    pallas_call x0 -> x5, Pallas kernels: none -> 22.5 us  [the longest x1 10.4 us: own(): pl.pallas_call(functools.partial(own_kernel, scale, block), out_shape=[sd...]
    all_to_all x2 -> x4, blocking collectives: 64.5 us -> 85.8 us  [exchange(): lax.all_to_all(piece, axes, split_axis=0, concat_axis=0, tiled=True)]
    dot_general x7 -> x0, matrix products: 17.7 us -> none  [the longest x1 5.43 us: per_device(): linear = jnp.dot(block, mine, precision=hp)]
    all_to_all x2, waiting for transfers between devices: 50.4 us -> 32.8 us  [exchange(): lax.all_to_all(piece, axes, split_axis=0, concat_axis=0, tiled=True)]
    all_to_all x2, starting transfers between devices: 16.1 us -> 8.4 us  [exchange(): lax.all_to_all(piece, axes, split_axis=0, concat_axis=0, tiled=True)]
    ppermute x1, starting transfers between devices: 5.66 us -> 0.01 us  [per_device(): theirs = lax.ppermute(mine, 'core', [(0, 1), (1, 0)])]
    cond x0 -> x10, local copies, waits for them, and re-layouts: none -> 3.8 us
    dot_general x2 -> x0, local copies, waits for them, and re-layouts: 3.75 us -> none  [mix_rows(): jnp.einsum('dc,cph->dph', table, blocks, precision=lax.Precision.HIGH)]
  transfers between devices with their start and end apart: 3 -> 3, of which waited for: 2 -> 2; matrix products, arithmetic and copies ran while one was open for 9% -> 2% of each run, Pallas kernels for 0% -> 6%
where the time goes in v2:
time: 165 us
  blocking collectives  85.8 us (52%)
  waiting for transfers between devices  32.8 us (20%)
  Pallas kernels  22.5 us (14%)
  local copies, waits for them, and re-layouts  12.6 us (8%)
  starting transfers between devices  8.4 us (5%)
  other arithmetic  2.2 us (1%)
    all_to_all x4, blocking collectives, exchange(): lax.all_to_all(piece, axes, split_axis=0, concat_axis=0, tiled=True)  85.8 us
    all_to_all x2, waiting for transfers between devices, exchange(): lax.all_to_all(piece, axes, split_axis=0, concat_axis=0, tiled=True)  32.8 us
    pallas_call x1, Pallas kernels, own(): pl.pallas_call(functools.partial(own_kernel, scale, block), out_shape=[sd...  10.4 us
    all_to_all x2, starting transfers between devices, exchange(): lax.all_to_all(piece, axes, split_axis=0, concat_axis=0, tiled=True)  8.4 us
    unnamed x6, local copies, waits for them, and re-layouts  7.09 us
    pallas_call x2, Pallas kernels, mix(): pl.pallas_call(mix_kernel, out_shape=jax.ShapeDtypeStruct((n, part, width...  5.34 us
    pallas_call x1, Pallas kernels, other(): pl.pallas_call(functools.partial(other_kernel, scale, cuts), out_shape=[j...  4.36 us
    cond x10, local copies, waits for them, and re-layouts  3.8 us
  transfers between devices with their start and end apart: 3, of which 2 were waited for; matrix products, arithmetic and copies ran while one was open for 2% of the time, Pallas kernels for 6%

profile of v2, /device:TPU:1, one launch (start us, length us, event | category | flops | bytes accessed | tf_op | source)
XLA Modules:
  0.0 164.7 jit_solution(17604646959035737459)
XLA Ops:
  0.0 77.4 %conditional.2 = (f32[64,64,128]{2,1,0:T(8,128)}, f32[64,64]{1,0:T(8,128)}) conditional(s32[]{:T(128)} %convert_element_type.4, (s32[64,64]{1,0:T(8,128)}, f32[64]{0:T(128)}, f32[4,1024,128]{2,1,0:T(8,128)}) %tuple.19, (s32[64,64]{1,0:T(8,128)}, f32[64]{0:T(128)}, f32[4,1024,128]{2,1,0:T(8,128)}) %tuple.19), branch_computations={%region_0.2_spmd, %region_2.4_spmd} | conditional | flops 1611395072 | bytes 26051972 | solution.py:226
  0.0 2.4 %branch_0_fun.4 = (f32[16,4,8,128]{3,2,1,0:T(8,128)S(1)}, f32[16,4,56,128]{3,2,1,0:T(8,128)S(1)}) custom-call(f32[4,16,64,128]{3,2,1,0:T(8,128)} %bitcast.22), custom_call_target="tpu_custom_call" | custom-call | bytes 4194304 | tf_op jit(solution)/shard_map/cond/branch_0_fun/pallas_call | solution.py:45
  2.4 0.0 copy-start.1
  2.4 1.2 copy-done.1
  3.6 14.9 %all_to_all.40.refs_0_ = f32[64,8,128]{2,1,0:T(8,128)S(1)} all-to-all(f32[64,8,128]{2,1,0:T(8,128)S(1)} %bitcast.19), channel_id=1, replica_groups=mesh['chan'=16,'z'=4,'core'=2] {'chan'}, dimensions={0} | all-to-all | bytes 524288 | tf_op jit(solution)/shard_map/cond/branch_0_fun/all_to_all | solution.py:192
  18.5 3.7 %all-to-all-start.1 = ((f32[64,56,128]{2,1,0:T(8,128)}), f32[64,56,128]{2,1,0:T(8,128)S(1)}, u32[]{:S(2)}, u32[]{:S(2)}) async-start(f32[64,56,128]{2,1,0:T(8,128)} %bitcast.18), calls=%async_computation.1 | async-start | bytes 3670016 | tf_op jit(solution)/shard_map/cond/branch_0_fun/all_to_all | solution.py:192
  22.3 0.0 copy-done.7
  22.3 0.0 copy-done.9
  22.3 1.9 %select_reduce_fusion.table = f32[64,64]{1,0:T(8,128)} fusion(f32[64]{0:T(128)S(1)} %copy-done.9, s32[64,64]{1,0:T(8,128)S(1)} %copy-done.7), kind=kLoop, calls=%fused_computation | loop fusion | flops 782336 | bytes 33024 | tf_op jit(solution)/shard_map/cond/branch_0_fun/reduce_sum | solution.py:197
  24.2 16.0 %all-to-all-done.1.refs_1_ = f32[64,56,128]{2,1,0:T(8,128)S(1)} async-done(((f32[64,56,128]{2,1,0:T(8,128)}), f32[64,56,128]{2,1,0:T(8,128)S(1)}, u32[]{:S(2)}, u32[]{:S(2)}) %all-to-all-start.1) | async-done | bytes 1835040 | tf_op jit(solution)/shard_map/cond/branch_0_fun/all_to_all | solution.py:192
  40.2 3.1 %branch_0_fun.5 = f32[64,64,128]{2,1,0:T(8,128)S(1)} custom-call(f32[64,64]{1,0:T(8,128)} %select_reduce_fusion.table, f32[64,8,128]{2,1,0:T(8,128)S(1)} %all_to_all.40.refs_0_, f32[64,56,128]{2,1,0:T(8,128)S(1)} %all-to-all-done.1.refs_1_), custom_call_target="tpu_custom_call" | custom-call | flops 1610612736 | bytes 4194304 | tf_op jit(solution)/shard_map/cond/branch_0_fun/pallas_call | solution.py:88
  43.3 34.1 %all_to_all.41 = f32[64,64,128]{2,1,0:T(8,128)} all-to-all(f32[64,64,128]{2,1,0:T(8,128)S(1)} %branch_0_fun.5), channel_id=1, replica_groups=mesh['chan'=16,'z'=4,'core'=2] {'chan','z'}, dimensions={0} | all-to-all | bytes 4194304 | tf_op jit(solution)/shard_map/cond/branch_0_fun/all_to_all | solution.py:192
  77.4 0.0 collective-permute-start
  77.4 0.6 dynamic_slice.3.rows
  78.0 5.8 %copy-done.3 = f32[4,1024,1024]{2,1,0:T(8,128)S(1)} copy-done((f32[4,1024,1024]{2,1,0:T(8,128)S(1)}, f32[4,1024,1024]{2,1,0:T(8,128)}, u32[]{:S(2)}) %copy-start.3) | copy-done | bytes 16777240
  83.8 10.4 %shard_map.68 = (f32[1024,512]{1,0:T(8,128)S(1)}, bf16[1024,512]{1,0:T(8,128)(2,1)S(1)}, bf16[1024,512]{1,0:T(8,128)(2,1)S(1)}) custom-call(s32[1]{0:T(128)} %bitcast.15.at, s32[1]{0:T(128)} %dynamic_slice.3.rows, f32[64,64,128]{2,1,0:T(8,128)} %get-tuple-element.78.side, f32[4,1024,1024]{2,1,0:T(8,128)S(1)} %copy-done.3), custom_call_target="tpu_custom_call" | custom-call | flops 6442450944 | bytes 10485760 | tf_op jit(solution)/shard_map/pallas_call | solution.py:137
  94.2 0.0 collective-permute-done
  94.2 69.1 %conditional.3 = (f32[4,1024,128]{2,1,0:T(8,128)S(1)}) conditional(s32[]{:T(128)} %convert_element_type.4, (f32[64,64]{1,0:T(8,128)}, s32[1]{0:T(128)}, f32[64,64,128]{2,1,0:T(8,128)S(1)}, f32[1024,512]{1,0:T(8,128)S(1)}, bf16[1024,512]{1,0:T(8,128)(2,1)S(1)}, /*index=5*/bf16[1024,512]{1,0:T(8,128)(2,1)S(1)}, f32[4,1024,128]{2,1,0:T(8,128)}) %tuple.20, ...), branch_computations={%region_4.5_spmd, %region_5.6_spmd} | conditional | flops 4832362496 | bytes 50364512 | solution.py:229
  94.2 4.4 %branch_0_fun.6 = (f32[64,8,128]{2,1,0:T(8,128)S(1)}, f32[64,56,128]{2,1,0:T(8,128)S(1)}) custom-call(s32[1]{0:T(128)} %get-tuple-element.57.rows, f32[64,64,128]{2,1,0:T(8,128)S(1)} %get-tuple-element.58.side, f32[1024,512]{1,0:T(8,128)S(1)} %get-tuple-element.59.base, bf16[1024,512]{1,0:T(8,128)(2,1)S(1)} %get-tuple-element.60.lin_h, ...), custom_call_target="tpu_custom_call" | custom-call | flops 3221225472 | bytes 8388608 | tf_op jit(solution)/shard_map/cond/branch_0_fun/pallas_call | solution.py:178
  98.6 0.0 copy-start.2
  98.6 1.2 copy-done.2
  99.8 15.4 %all_to_all.43.refs_0_ = f32[64,8,128]{2,1,0:T(8,128)S(1)} all-to-all(f32[64,8,128]{2,1,0:T(8,128)S(1)} %get-tuple-element.62), channel_id=1, replica_groups=mesh['chan'=16,'z'=4,'core'=2] {'chan','z'}, dimensions={0} | all-to-all | bytes 524288 | tf_op jit(solution)/shard_map/cond/branch_0_fun/all_to_all | solution.py:192
  115.2 4.7 %all-to-all-start.6 = ((f32[64,56,128]{2,1,0:T(8,128)}), f32[64,56,128]{2,1,0:T(8,128)S(1)}, u32[]{:S(2)}, u32[]{:S(2)}) async-start(f32[64,56,128]{2,1,0:T(8,128)} %copy-done.2), calls=%async_computation.6 | async-start | bytes 3670016 | tf_op jit(solution)/shard_map/cond/branch_0_fun/all_to_all | solution.py:192
  119.9 0.8 copy.17
  120.7 16.7 %all-to-all-done.6.refs_1_ = f32[64,56,128]{2,1,0:T(8,128)S(1)} async-done(((f32[64,56,128]{2,1,0:T(8,128)}), f32[64,56,128]{2,1,0:T(8,128)S(1)}, u32[]{:S(2)}, u32[]{:S(2)}) %all-to-all-start.6) | async-done | bytes 1835040 | tf_op jit(solution)/shard_map/cond/branch_0_fun/all_to_all | solution.py:192
  137.5 2.3 %branch_0_fun.7 = f32[64,64,128]{2,1,0:T(8,128)S(1)} custom-call(f32[64,64]{1,0:T(8,128)S(1)} %bitcast.20, f32[64,8,128]{2,1,0:T(8,128)S(1)} %all_to_all.43.refs_0_, f32[64,56,128]{2,1,0:T(8,128)S(1)} %all-to-all-done.6.refs_1_), custom_call_target="tpu_custom_call" | custom-call | flops 1610612736 | bytes 4194304 | tf_op jit(solution)/shard_map/cond/branch_0_fun/pallas_call | solution.py:88
  139.8 21.5 %all_to_all.44 = f32[64,64,128]{2,1,0:T(8,128)S(1)} all-to-all(f32[64,64,128]{2,1,0:T(8,128)S(1)} %branch_0_fun.7), channel_id=1, replica_groups=mesh['chan'=16,'z'=4,'core'=2] {'chan'}, dimensions={0} | all-to-all | bytes 4194304 | tf_op jit(solution)/shard_map/cond/branch_0_fun/all_to_all | solution.py:192
  161.2 0.2 copy.15
  161.5 1.3 copy-done.4
  162.8 0.3 bitcast_divide_fusion
  163.3 0.0 copy-start.6
  163.3 1.3 copy-done.6
  (6 shorter events, 0.0 us)
Async XLA Ops:
  0.0 77.4 %copy-start.11 = (s32[4]{0:T(128)S(1)}, s32[4]{0:T(128)}, u32[]{:S(2)}) copy-start(s32[4]{0:T(128)} %param.14) | copy-start | bytes 52
  2.4 1.2 copy-start.1
  3.6 18.6 %copy-start.7 = (s32[64,64]{1,0:T(8,128)S(1)}, s32[64,64]{1,0:T(8,128)}, u32[]{:S(2)}) copy-start(s32[64,64]{1,0:T(8,128)} %get-tuple-element.48) | copy-start | bytes 49156 | tf_op jit(solution)/shard_map/cond
  3.6 18.6 %copy-start.9 = (f32[64]{0:T(128)S(1)}, f32[64]{0:T(128)}, u32[]{:S(2)}) copy-start(f32[64]{0:T(128)} %get-tuple-element.49) | copy-start | bytes 772 | tf_op jit(solution)/shard_map/cond
  18.5 21.7 %all-to-all-start.1 = ((f32[64,56,128]{2,1,0:T(8,128)}), f32[64,56,128]{2,1,0:T(8,128)S(1)}, u32[]{:S(2)}, u32[]{:S(2)}) async-start(f32[64,56,128]{2,1,0:T(8,128)} %bitcast.18), calls=%async_computation.1 | async-start | bytes 3670016 | tf_op jit(solution)/shard_map/cond/branch_0_fun/all_to_all | solution.py:192
  77.4 16.8 %collective-permute-start = (f32[64,64,128]{2,1,0:T(8,128)}, f32[64,64,128]{2,1,0:T(8,128)S(1)}, u32[]{:S(2)}, u32[]{:S(2)}) collective-permute-start(f32[64,64,128]{2,1,0:T(8,128)} %get-tuple-element.78.side), channel_id=1, source_target_pairs={{0,1},{1,0},{2,3},{3,2},{4,5},{5,4},{6,7},{7,6},{8,9},{9,8},{10,11... | collective-permute-start | bytes 6291464 | tf_op jit(solution)/shard_map/ppermute | solution.py:227
  78.0 5.8 %copy-start.3 = (f32[4,1024,1024]{2,1,0:T(8,128)S(1)}, f32[4,1024,1024]{2,1,0:T(8,128)}, u32[]{:S(2)}) copy-start(f32[4,1024,1024]{2,1,0:T(8,128)} %inter.1) | copy-start | bytes 50331652
  98.6 1.2 copy-start.2
  115.2 22.3 %all-to-all-start.6 = ((f32[64,56,128]{2,1,0:T(8,128)}), f32[64,56,128]{2,1,0:T(8,128)S(1)}, u32[]{:S(2)}, u32[]{:S(2)}) async-start(f32[64,56,128]{2,1,0:T(8,128)} %copy-done.2), calls=%async_computation.6 | async-start | bytes 3670016 | tf_op jit(solution)/shard_map/cond/branch_0_fun/all_to_all | solution.py:192
  161.2 1.6 copy-start.4
  163.3 1.3 copy-start.6

commit v3 on v2

--- a/solution.py
+++ b/solution.py
@@ -1,3 +1,4 @@
+import bisect
 import functools
 import jax
 import jax.numpy as jnp
@@ -7,7 +8,12 @@
 from jax.sharding import Mesh, PartitionSpec as P
 
 CHIPS = ("chan", "z")
-WHOLE, SPLIT = (0, 64), (0, 8, 64)
+FIRST = ((0, 64), (0, 8, 64))
+THIRD = ((0, 64), (0, 8, 64))
+OWN_MIB = 52
+EARLY1 = (False, False)
+EARLY = (True, True)
+LAST = ((0, 64), (0, 64))
 MIB = 2**20
 BF16, F32 = jnp.bfloat16, jnp.float32
 ANY = pl.BlockSpec(memory_space=pl.ANY)
@@ -32,22 +38,31 @@
     return pltpu.CompilerParams(vmem_limit_bytes=mib * MIB)
 
 
-def deal_kernel(cuts, blocks, *outs):
-    for c in range(blocks.shape[0]):
-        for k, out in enumerate(outs):
-            out[:, c] = blocks[c, :, cuts[k] : cuts[k + 1]]
-
-
-def deal(blocks, n, cuts, step=4):
+def deal_kernel(cuts, blocks, *refs):
+    outs, sems = refs[:-1], refs[-1]
+    copies = [
+        pltpu.make_async_copy(
+            blocks.at[c, :, pl.ds(cuts[k], cuts[k + 1] - cuts[k])], out.at[:, c], sems.at[k * blocks.shape[0] + c]
+        )
+        for k, out in enumerate(outs)
+        for c in range(blocks.shape[0])
+    ]
+    for copy in copies:
+        copy.start()
+    for copy in copies:
+        copy.wait()
+
+
+def deal(blocks, n, cuts):
     c, height, width = blocks.shape
     part = height // n
     sizes = [b - a for a, b in zip(cuts[:-1], cuts[1:])]
     pieces = pl.pallas_call(
         functools.partial(deal_kernel, cuts),
-        grid=(n // step,),
         out_shape=[jax.ShapeDtypeStruct((n, c, rows, width), F32) for rows in sizes],
-        in_specs=[pl.BlockSpec((c, step, part, width), lambda i: (0, i, 0, 0))],
-        out_specs=[pl.BlockSpec((step, c, rows, width), lambda i: (i, 0, 0, 0)) for rows in sizes],
+        in_specs=[ANY],
+        out_specs=[FULL] * len(sizes),
+        scratch_shapes=[pltpu.SemaphoreType.DMA((len(sizes) * c,))],
         compiler_params=params(8),
         cost_estimate=pl.CostEstimate(flops=0, bytes_accessed=8 * c * height * width, transcendentals=0),
     )(blocks.reshape(c, n, part, width))
@@ -68,10 +83,16 @@
     return tuple(spread)
 
 
-def mix_kernel(table, *refs):
-    ins, out = refs[:-1], refs[-1]
-    n, _, width = out.shape
-    spread = spread_table(table[...])
+def mix_kernel(cuts, back, values, index, *refs):
+    ins, outs = refs[: 1 - len(cuts)], refs[1 - len(cuts) :]
+    n, _, width = outs[0].shape
+    if values.shape == index.shape:
+        table = values[...]
+    else:
+        table = jnp.zeros(index.shape, F32)
+        for slot in range(values.shape[0]):
+            table = jnp.where(index[...] == slot, values[slot], table)
+    spread = spread_table(table.T if back else table)
     groups = [(ref, row) for ref in ins for row in range(0, ref.shape[1], SUB)]
     for at in range(0, len(groups), 2):
         x = jnp.concatenate(
@@ -79,22 +100,24 @@
         )
         y = dot3(spread, halves(x))
         for k in range(2):
-            out[:, (at + k) * SUB : (at + k + 1) * SUB, :] = y[:, k * width : (k + 1) * width].reshape(n, SUB, width)
-
-
-def mix(table, pieces):
+            row = (at + k) * SUB
+            i = bisect.bisect_right(cuts, row) - 1
+            outs[i][:, row - cuts[i] : row - cuts[i] + SUB, :] = y[:, k * width : (k + 1) * width].reshape(n, SUB, width)
+
+
+def mix(values, index, pieces, cuts, back=False):
     n, _, width = pieces[0].shape
-    part = sum(p.shape[1] for p in pieces)
-    return pl.pallas_call(
-        mix_kernel,
-        out_shape=jax.ShapeDtypeStruct((n, part, width), F32),
-        in_specs=[FULL] * (1 + len(pieces)),
-        out_specs=FULL,
+    part = cuts[-1]
+    return pl.pallas_call(
+        functools.partial(mix_kernel, cuts, back),
+        out_shape=[jax.ShapeDtypeStruct((n, b - a, width), F32) for a, b in zip(cuts[:-1], cuts[1:])],
+        in_specs=[FULL if values.ndim == 2 else SCALAR] + [FULL] * (1 + len(pieces)),
+        out_specs=[FULL] * (len(cuts) - 1),
         compiler_params=params(16),
         cost_estimate=pl.CostEstimate(
             flops=6 * n * n * part * width * SUB, bytes_accessed=8 * n * part * width, transcendentals=0
         ),
-    )(table, *pieces)
+    )(values, index, *pieces)
 
 
 def gather_side(ref, rows_of, scratch_high, scratch_low):
@@ -109,15 +132,18 @@
             scratch_low[span, k * width : (k + 1) * width] = low
 
 
-def own_kernel(scale, block, at, rows, side, inter, acc, lin_h, lin_l, v, side_h, side_l, sem):
+def own_kernel(scale, block, at, rows, side, inter, acc, lin_h, lin_l, v, raw, side_h, side_l, sem):
     height = v.shape[0]
+    first = pltpu.make_async_copy(side, raw, sem.at[0])
+    first.start()
     copies = [
-        pltpu.make_async_copy(inter.at[at[0], pl.ds(r, block)], v.at[pl.ds(r, block)], sem.at[r // block])
+        pltpu.make_async_copy(inter.at[at[0], pl.ds(r, block)], v.at[pl.ds(r, block)], sem.at[1 + r // block])
         for r in range(0, height, block)
     ]
     for copy in copies:
         copy.start()
-    gather_side(side, rows[0], side_h, side_l)
+    first.wait()
+    gather_side(raw, rows[0], side_h, side_l)
     mine = (side_h[...], side_l[...])
     for r, copy in zip(range(0, height, block), copies):
         copy.wait()
@@ -137,15 +163,16 @@
     return pl.pallas_call(
         functools.partial(own_kernel, scale, block),
         out_shape=[sds((height, cols), F32), sds((height, cols), BF16), sds((height, cols), BF16)],
-        in_specs=[SCALAR, SCALAR, FULL, ANY],
+        in_specs=[SCALAR, SCALAR, ANY, ANY],
         out_specs=[FULL] * 3,
         scratch_shapes=[
             pltpu.VMEM((height, height), F32),
+            pltpu.VMEM(side.shape, F32),
             pltpu.VMEM((height, cols), BF16),
             pltpu.VMEM((height, cols), BF16),
-            pltpu.SemaphoreType.DMA((height // block,)),
+            pltpu.SemaphoreType.DMA((1 + height // block,)),
         ],
-        compiler_params=params(30),
+        compiler_params=params(OWN_MIB),
         cost_estimate=pl.CostEstimate(
             flops=12 * height * height * cols, bytes_accessed=4 * height * (height + 3 * cols), transcendentals=0
         ),
@@ -188,6 +215,29 @@
     )(rows, side, base, lin_h, lin_l)
 
 
+def finish_kernel(cuts, below, *refs):
+    ins, out = refs[:-1], refs[-1]
+    for i, ref in enumerate(ins):
+        rows = slice(cuts[i], cuts[i + 1])
+        out[0, :, rows] = ref[:, 0] / below[0, :, rows]
+
+
+def finish(pieces, below, n, cuts):
+    c, height, width = below.shape
+    part = height // n
+    whole = pl.BlockSpec((1, n, part, width), lambda i: (i, 0, 0, 0))
+    sizes = [b - a for a, b in zip(cuts[:-1], cuts[1:])]
+    return pl.pallas_call(
+        functools.partial(finish_kernel, cuts),
+        grid=(c,),
+        out_shape=jax.ShapeDtypeStruct((c, n, part, width), F32),
+        in_specs=[whole] + [pl.BlockSpec((n, 1, rows, width), lambda i: (0, i, 0, 0)) for rows in sizes],
+        out_specs=whole,
+        compiler_params=params(12),
+        cost_estimate=pl.CostEstimate(flops=c * height * width, bytes_accessed=12 * c * height * width, transcendentals=0),
+    )(below.reshape(c, n, part, width), *[p.reshape(n, c, rows, width) for p, rows in zip(pieces, sizes)]).reshape(c, height, width)
+
+
 def exchange(pieces, axes):
     return [lax.all_to_all(piece, axes, split_axis=0, concat_axis=0, tiled=True) for piece in pieces]
 
@@ -205,30 +255,30 @@
     rows_of = lax.dynamic_slice_in_dim(ph_rows, z, 1)
     scale = 1.0 / (height * width * n_z * 2) ** 0.5
 
-    def forward(cuts):
+    def forward(core):
         def run(blocks, values, index):
-            weights = weights_of(values, index)
-            mixed = mix(weights, exchange(deal(blocks, n_chan, cuts), "chan"))
-            return exchange([mixed], CHIPS)[0], weights
+            parts = exchange(deal(blocks, n_chan, FIRST[core]), "chan")
+            if EARLY1[core]:
+                values = weights_of(values, index)
+            return exchange(mix(values, index, parts, (0, height // n_chan)), CHIPS)[0]
 
         return run
 
-    def backward(cuts):
-        def run(rows, theirs, base, lin_h, lin_l, weights, below):
-            cycle = other(rows, theirs, base, lin_h, lin_l, scale, cuts)
-            back = mix(weights.T, exchange(cycle, CHIPS))
-            back = exchange([back], "chan")[0]
-            back = back.reshape(n_chan, c, height // n_chan, width).transpose(1, 0, 2, 3).reshape(c, height, width)
-            return back / below
+    def backward(core):
+        def run(rows, theirs, values, index, below, *sums):
+            cycle = other(rows, theirs, *sums, scale, THIRD[core])
+            if EARLY[core]:
+                values = weights_of(values, index)
+            back = mix(values, index, exchange(cycle, CHIPS), LAST[core], back=True)
+            return finish(exchange(back, "chan"), below, n_chan, LAST[core])
 
         return run
 
-    mine, weights = lax.cond(core == 0, forward(WHOLE), forward(SPLIT), amplitudes, sixj_values, sixj_index)
+    tables = (sixj_values, sixj_index)
+    mine = lax.cond(core == 0, forward(0), forward(1), amplitudes, *tables)
     theirs = lax.ppermute(mine, "core", [(0, 1), (1, 0)])
-    base, lin_h, lin_l = own(at, rows_of, mine, interaction, scale)
-    return lax.cond(
-        core == 0, backward(WHOLE), backward(SPLIT), rows_of, theirs, base, lin_h, lin_l, weights, denominators
-    )
+    sums = own(at, rows_of, mine, interaction, scale)
+    return lax.cond(core == 0, backward(0), backward(1), rows_of, theirs, *tables, denominators, *sums)
 
 
 def solution(mesh):

time: 165 us -> 152 us (0.921)
  blocking collectives: 85.8 us -> 103 us
  waiting for transfers between devices: 32.8 us -> 16.1 us
  local copies, waits for them, and re-layouts: 12.6 us -> 3.14 us
  starting transfers between devices: 8.4 us -> 4.69 us
    all_to_all x4 -> x5, blocking collectives: 85.8 us -> 103 us  [exchange(): lax.all_to_all(piece, axes, split_axis=0, concat_axis=0, tiled=True)]
    all_to_all x2 -> x1, waiting for transfers between devices: 32.8 us -> 16.1 us  [exchange(): lax.all_to_all(piece, axes, split_axis=0, concat_axis=0, tiled=True)]
    unnamed x6 -> x8, local copies, waits for them, and re-layouts: 7.09 us -> 1.32 us
    all_to_all x2 -> x1, starting transfers between devices: 8.4 us -> 4.69 us  [exchange(): lax.all_to_all(piece, axes, split_axis=0, concat_axis=0, tiled=True)]
    cond x10 -> x8, local copies, waits for them, and re-layouts: 3.8 us -> 1.24 us
    pallas_call x3 -> x4, Pallas kernels: 7.73 us -> 7.54 us  [the longest x2 5.35 us: mix(): pl.pallas_call(functools.partial(mix_kernel, cuts, back), out_shape=[jax....]
  transfers between devices with their start and end apart: 3 -> 2, of which waited for: 2 -> 1; matrix products, arithmetic and copies ran while one was open for 2% -> 1% of each run, Pallas kernels for 6% -> 6%
where the time goes in v3:
time: 152 us
  blocking collectives  103 us (68%)
  Pallas kernels  22.8 us (15%)
  waiting for transfers between devices  16.1 us (11%)
  starting transfers between devices  4.69 us (3%)
  local copies, waits for them, and re-layouts  3.14 us (2%)
    all_to_all x5, blocking collectives, exchange(): lax.all_to_all(piece, axes, split_axis=0, concat_axis=0, tiled=True)  103 us
    all_to_all x1, waiting for transfers between devices, exchange(): lax.all_to_all(piece, axes, split_axis=0, concat_axis=0, tiled=True)  16.1 us
    pallas_call x1, Pallas kernels, own(): pl.pallas_call(functools.partial(own_kernel, scale, block), out_shape=[sd...  9.32 us
    pallas_call x1, Pallas kernels, other(): pl.pallas_call(functools.partial(other_kernel, scale, cuts), out_shape=[j...  5.91 us
    pallas_call x2, Pallas kernels, mix(): pl.pallas_call(functools.partial(mix_kernel, cuts, back), out_shape=[jax....  5.35 us
    all_to_all x1, starting transfers between devices, exchange(): lax.all_to_all(piece, axes, split_axis=0, concat_axis=0, tiled=True)  4.69 us
  transfers between devices with their start and end apart: 2, of which 1 were waited for; matrix products, arithmetic and copies ran while one was open for 1% of the time, Pallas kernels for 6%

profile of v3, /device:TPU:1, one launch (start us, length us, event | category | flops | bytes accessed | tf_op | source)
XLA Modules:
  0.0 151.9 jit_solution(1638275046505057506)
XLA Ops:
  0.0 71.5 %conditional.2 = (f32[64,64,128]{2,1,0:T(8,128)S(1)}) conditional(s32[]{:T(128)} %convert_element_type.4, (f32[4,1024,128]{2,1,0:T(8,128)}, f32[64]{0:T(128)}, s32[64,64]{1,0:T(8,128)}) %tuple.17, (f32[4,1024,128]{2,1,0:T(8,128)}, f32[64]{0:T(128)}, s32[64,64]{1,0:T(8,128)}) %tuple.17), branch_computations={%region_0.0_spmd, %region_1.0_spmd} | conditional | flops 1610612736 | bytes 16843840 | solution.py:278
  0.0 1.7 %branch_0_fun.5 = (f32[16,4,8,128]{3,2,1,0:T(8,128)S(1)}, f32[16,4,56,128]{3,2,1,0:T(8,128)S(1)}) custom-call(f32[4,16,64,128]{3,2,1,0:T(8,128)} %bitcast.19), custom_call_target="tpu_custom_call" | custom-call | bytes 4194304 | tf_op jit(solution)/shard_map/cond/branch_0_fun/pallas_call | solution.py:60
  1.7 0.0 copy-start.6
  1.7 0.0 copy-start.9
  1.7 14.9 %all_to_all.40.refs_0_ = f32[64,8,128]{2,1,0:T(8,128)S(1)} all-to-all(f32[64,8,128]{2,1,0:T(8,128)S(1)} %bitcast.16), channel_id=1, replica_groups=mesh['chan'=16,'z'=4,'core'=2] {'chan'}, dimensions={0} | all-to-all | bytes 524288 | tf_op jit(solution)/shard_map/cond/branch_0_fun/all_to_all | solution.py:242
  16.6 20.9 %all_to_all.41.refs_1_ = f32[64,56,128]{2,1,0:T(8,128)S(1)} all-to-all(f32[64,56,128]{2,1,0:T(8,128)S(1)} %bitcast.15), channel_id=1, replica_groups=mesh['chan'=16,'z'=4,'core'=2] {'chan'}, dimensions={0} | all-to-all | bytes 3670016 | tf_op jit(solution)/shard_map/cond/branch_0_fun/all_to_all | solution.py:242
  37.5 0.0 copy-done.6
  37.5 0.0 copy-done.9
  37.5 3.0 %branch_0_fun.6 = f32[64,64,128]{2,1,0:T(8,128)S(1)} custom-call(f32[64]{0:T(128)S(1)} %copy-done.9, s32[64,64]{1,0:T(8,128)S(1)} %copy-done.6, f32[64,8,128]{2,1,0:T(8,128)S(1)} %all_to_all.40.refs_0_, f32[64,56,128]{2,1,0:T(8,128)S(1)} %all_to_all.41.refs_1_), custom_call_target="tpu_custom_call" | custom-call | flops 1610612736 | bytes 4194304 | tf_op jit(solution)/shard_map/cond/branch_0_fun/pallas_call | solution.py:111
  40.5 31.0 %all_to_all.42 = f32[64,64,128]{2,1,0:T(8,128)S(1)} all-to-all(f32[64,64,128]{2,1,0:T(8,128)S(1)} %branch_0_fun.6), channel_id=1, replica_groups=mesh['chan'=16,'z'=4,'core'=2] {'chan','z'}, dimensions={0} | all-to-all | bytes 4194304 | tf_op jit(solution)/shard_map/cond/branch_0_fun/all_to_all | solution.py:242
  71.5 0.0 collective-permute-start
  71.5 0.0 copy-done.11
  71.5 0.6 dynamic_slice.3.rows
  72.1 9.3 %shard_map.68 = (f32[1024,512]{1,0:T(8,128)S(1)}, bf16[1024,512]{1,0:T(8,128)(2,1)S(1)}, bf16[1024,512]{1,0:T(8,128)(2,1)S(1)}) custom-call(s32[1]{0:T(128)} %bitcast.11.at, s32[1]{0:T(128)} %dynamic_slice.3.rows, f32[64,64,128]{2,1,0:T(8,128)S(1)} %get-tuple-element.94.side, f32[4,1024,1024]{2,1,0:T(8,128)} %inter.1), custom_call_target="tpu_custom_call" | custom-call | flops 6442450944 | bytes 10485760 | tf_op jit(solution)/shard_map/pallas_call | solution.py:163
  81.4 0.0 collective-permute-done
  81.4 0.0 copy-done.5
  81.4 0.0 copy-done.8
  81.4 69.1 %conditional.3 = (f32[4,1024,128]{2,1,0:T(8,128)S(1)}) conditional(s32[]{:T(128)} %convert_element_type.4, (f32[4,1024,128]{2,1,0:T(8,128)}, s32[64,64]{1,0:T(8,128)S(1)}, f32[64]{0:T(128)S(1)}, s32[1]{0:T(128)}, f32[64,64,128]{2,1,0:T(8,128)}, /*index=5*/f32[1024,512]{1,0:T(8,128)S(1)}, bf16[1024,512]{1,0:T(8,128)(2,1)S(1)}, ...), branch_computations={%region_2.4_spmd, %region_4.6_spmd} | conditional | flops 4833144832 | bytes 46170464 | solution.py:281
  81.6 5.9 %branch_0_fun.7 = (f32[64,8,128]{2,1,0:T(8,128)S(1)}, f32[64,56,128]{2,1,0:T(8,128)S(1)}) custom-call(s32[1]{0:T(128)} %get-tuple-element.66.rows, f32[64,64,128]{2,1,0:T(8,128)} %get-tuple-element.67.side, f32[1024,512]{1,0:T(8,128)S(1)} %get-tuple-element.68.base, bf16[1024,512]{1,0:T(8,128)(2,1)S(1)} %get-tuple-element.69.lin_h, ...), custom_call_target="tpu_custom_call" | custom-call | flops 3221225472 | bytes 8388608 | tf_op jit(solution)/shard_map/cond/branch_0_fun/pallas_call | solution.py:205
  87.5 0.0 copy-start.1
  87.6 1.2 copy-done.1
  88.8 15.1 %all_to_all.45.refs_0_ = f32[64,8,128]{2,1,0:T(8,128)S(1)} all-to-all(f32[64,8,128]{2,1,0:T(8,128)S(1)} %get-tuple-element.71), channel_id=1, replica_groups=mesh['chan'=16,'z'=4,'core'=2] {'chan','z'}, dimensions={0} | all-to-all | bytes 524288 | tf_op jit(solution)/shard_map/cond/branch_0_fun/all_to_all | solution.py:242
  103.8 4.7 %all-to-all-start.6 = ((f32[64,56,128]{2,1,0:T(8,128)}), f32[64,56,128]{2,1,0:T(8,128)S(1)}, u32[]{:S(2)}, u32[]{:S(2)}) async-start(f32[64,56,128]{2,1,0:T(8,128)} %copy-done.1), calls=%async_computation.6 | async-start | bytes 3670016 | tf_op jit(solution)/shard_map/cond/branch_0_fun/all_to_all | solution.py:242
  108.5 1.3 select_reduce_fusion.values
  109.8 16.1 %all-to-all-done.6.refs_1_ = f32[64,56,128]{2,1,0:T(8,128)S(1)} async-done(((f32[64,56,128]{2,1,0:T(8,128)}), f32[64,56,128]{2,1,0:T(8,128)S(1)}, u32[]{:S(2)}, u32[]{:S(2)}) %all-to-all-start.6) | async-done | bytes 1835040 | tf_op jit(solution)/shard_map/cond/branch_0_fun/all_to_all | solution.py:242
  125.9 2.4 %branch_0_fun.8 = f32[64,64,128]{2,1,0:T(8,128)S(1)} custom-call(f32[64,64]{1,0:T(8,128)S(1)} %select_reduce_fusion.values, s32[64,64]{1,0:T(8,128)S(1)} %get-tuple-element.64.index, f32[64,8,128]{2,1,0:T(8,128)S(1)} %all_to_all.45.refs_0_, f32[64,56,128]{2,1,0:T(8,128)S(1)} %all-to-all-done.6.refs_1_), custom_call_target="tpu_custom_call" | custom-call | flops 1610612736 | bytes 4194304 | tf_op jit(solution)/shard_map/cond/branch_0_fun/pallas_call | solution.py:111
  128.3 0.0 copy-start.2
  128.3 21.5 %all_to_all.46 = f32[64,64,128]{2,1,0:T(8,128)S(1)} all-to-all(f32[64,64,128]{2,1,0:T(8,128)S(1)} %branch_0_fun.8), channel_id=1, replica_groups=mesh['chan'=16,'z'=4,'core'=2] {'chan'}, dimensions={0} | all-to-all | bytes 4194304 | tf_op jit(solution)/shard_map/cond/branch_0_fun/all_to_all | solution.py:242
  149.8 0.0 copy-done.2
  149.8 0.5 branch_0_fun.9
  150.6 0.0 copy-start.4
  150.6 1.3 copy-done.4
  (3 shorter events, 0.0 us)
Async XLA Ops:
  0.0 71.5 %copy-start.11 = (s32[4]{0:T(128)S(1)}, s32[4]{0:T(128)}, u32[]{:S(2)}) copy-start(s32[4]{0:T(128)} %param.14) | copy-start | bytes 52
  1.7 35.8 %copy-start.6 = (s32[64,64]{1,0:T(8,128)S(1)}, s32[64,64]{1,0:T(8,128)}, u32[]{:S(2)}) copy-start(s32[64,64]{1,0:T(8,128)} %get-tuple-element.56.index) | copy-start | bytes 49156 | tf_op jit(solution)/shard_map/cond
  1.7 35.8 %copy-start.9 = (f32[64]{0:T(128)S(1)}, f32[64]{0:T(128)}, u32[]{:S(2)}) copy-start(f32[64]{0:T(128)} %get-tuple-element.54.values) | copy-start | bytes 772 | tf_op jit(solution)/shard_map/cond
  71.5 9.9 %collective-permute-start = (f32[64,64,128]{2,1,0:T(8,128)S(1)}, f32[64,64,128]{2,1,0:T(8,128)}, u32[]{:S(2)}, u32[]{:S(2)}) collective-permute-start(f32[64,64,128]{2,1,0:T(8,128)S(1)} %get-tuple-element.94.side), channel_id=1, source_target_pairs={{0,1},{1,0},{2,3},{3,2},{4,5},{5,4},{6,7},{7,6},{8,9},{9,8},{10,11... | collective-permute-start | bytes 6291464 | tf_op jit(solution)/shard_map/ppermute | solution.py:279
  72.1 9.3 %copy-start.5 = (s32[64,64]{1,0:T(8,128)S(1)}, s32[64,64]{1,0:T(8,128)}, u32[]{:S(2)}) copy-start(s32[64,64]{1,0:T(8,128)} %param.13) | copy-start | bytes 49156
  72.1 9.4 %copy-start.8 = (f32[64]{0:T(128)S(1)}, f32[64]{0:T(128)}, u32[]{:S(2)}) copy-start(f32[64]{0:T(128)} %param.12) | copy-start | bytes 772
  87.5 1.2 copy-start.1
  103.8 22.1 %all-to-all-start.6 = ((f32[64,56,128]{2,1,0:T(8,128)}), f32[64,56,128]{2,1,0:T(8,128)S(1)}, u32[]{:S(2)}, u32[]{:S(2)}) async-start(f32[64,56,128]{2,1,0:T(8,128)} %copy-done.1), calls=%async_computation.6 | async-start | bytes 3670016 | tf_op jit(solution)/shard_map/cond/branch_0_fun/all_to_all | solution.py:242
  128.3 21.5 %copy-start.2 = (f32[4,1024,128]{2,1,0:T(8,128)S(1)}, f32[4,1024,128]{2,1,0:T(8,128)}, u32[]{:S(2)}) copy-start(f32[4,1024,128]{2,1,0:T(8,128)} %get-tuple-element.90) | copy-start | bytes 6291460 | tf_op jit(solution)/shard_map/cond
  150.6 1.3 copy-start.4

commit v4 on v3

--- a/solution.py
+++ b/solution.py
@@ -11,8 +11,6 @@
 FIRST = ((0, 64), (0, 8, 64))
 THIRD = ((0, 64), (0, 8, 64))
 OWN_MIB = 52
-EARLY1 = (False, False)
-EARLY = (True, True)
 LAST = ((0, 64), (0, 64))
 MIB = 2**20
 BF16, F32 = jnp.bfloat16, jnp.float32
@@ -83,17 +81,20 @@
     return tuple(spread)
 
 
-def mix_kernel(cuts, back, values, index, *refs):
-    ins, outs = refs[: 1 - len(cuts)], refs[1 - len(cuts) :]
+def mix_kernel(cuts, back, *refs):
+    n_in, n_out = (1, len(cuts) - 1) if back else (2, len(cuts))
+    given, pieces, outs = refs[:n_in], refs[n_in:-n_out], refs[-n_out:]
     n, _, width = outs[0].shape
-    if values.shape == index.shape:
-        table = values[...]
+    if back:
+        table = given[0][...].T
     else:
+        values, index = given
         table = jnp.zeros(index.shape, F32)
         for slot in range(values.shape[0]):
             table = jnp.where(index[...] == slot, values[slot], table)
-    spread = spread_table(table.T if back else table)
-    groups = [(ref, row) for ref in ins for row in range(0, ref.shape[1], SUB)]
+        outs[-1][...] = table
+    spread = spread_table(table)
+    groups = [(ref, row) for ref in pieces for row in range(0, ref.shape[1], SUB)]
     for at in range(0, len(groups), 2):
         x = jnp.concatenate(
             [ref[:, row : row + SUB, :].reshape(n * SUB, width) for ref, row in groups[at : at + 2]], axis=1
@@ -105,19 +106,22 @@
             outs[i][:, row - cuts[i] : row - cuts[i] + SUB, :] = y[:, k * width : (k + 1) * width].reshape(n, SUB, width)
 
 
-def mix(values, index, pieces, cuts, back=False):
+def mix(given, pieces, cuts, back=False):
     n, _, width = pieces[0].shape
     part = cuts[-1]
+    shapes = [jax.ShapeDtypeStruct((n, b - a, width), F32) for a, b in zip(cuts[:-1], cuts[1:])]
+    if not back:
+        shapes.append(jax.ShapeDtypeStruct((n, n), F32))
     return pl.pallas_call(
         functools.partial(mix_kernel, cuts, back),
-        out_shape=[jax.ShapeDtypeStruct((n, b - a, width), F32) for a, b in zip(cuts[:-1], cuts[1:])],
-        in_specs=[FULL if values.ndim == 2 else SCALAR] + [FULL] * (1 + len(pieces)),
-        out_specs=[FULL] * (len(cuts) - 1),
+        out_shape=shapes,
+        in_specs=([FULL] if back else [SCALAR, FULL]) + [FULL] * len(pieces),
+        out_specs=[FULL] * len(shapes),
         compiler_params=params(16),
         cost_estimate=pl.CostEstimate(
             flops=6 * n * n * part * width * SUB, bytes_accessed=8 * n * part * width, transcendentals=0
         ),
-    )(values, index, *pieces)
+    )(*given, *pieces)
 
 
 def gather_side(ref, rows_of, scratch_high, scratch_low):
@@ -143,7 +147,7 @@
     for copy in copies:
         copy.start()
     first.wait()
-    gather_side(raw, rows[0], side_h, side_l)
+    gather_side(raw, rows[at[0]], side_h, side_l)
     mine = (side_h[...], side_l[...])
     for r, copy in zip(range(0, height, block), copies):
         copy.wait()
@@ -179,18 +183,18 @@
     )(at, rows, side, inter)
 
 
-def other_kernel(scale, cuts, rows, side, base, lin_h, lin_l, *refs):
+def other_kernel(scale, cuts, at, rows, side, base, lin_h, lin_l, *refs):
     outs, (side_h, side_l) = refs[:-2], refs[-2:]
     n, part, width = side.shape
     n_z = side_h.shape[1] // width
-    gather_side(side, rows[0], side_h, side_l)
+    gather_side(side, rows[at[0]], side_h, side_l)
     theirs = (side_h[...], side_l[...])
     inner = halves(dot3(theirs, (lin_h[...], lin_l[...]), ((0,), (0,))) * scale)
     step = 4
     for g0 in range(0, n // n_z, step):
         span = slice(g0 * part, (g0 + step) * part)
         total = base[span] + dot3(tuple(s[span] for s in theirs), inner)
-        live = g0 * part + lax.broadcasted_iota(jnp.int32, total.shape, 0) < rows[0]
+        live = g0 * part + lax.broadcasted_iota(jnp.int32, total.shape, 0) < rows[at[0]]
         total = jnp.where(live, total, 0.0)
         for g in range(step):
             for k in range(n_z):
@@ -199,20 +203,20 @@
                     out[(g0 + g) * n_z + k] = tile[cuts[i] : cuts[i + 1]]
 
 
-def other(rows, side, base, lin_h, lin_l, scale, cuts):
+def other(at, rows, side, base, lin_h, lin_l, scale, cuts):
     n, part, width = side.shape
     height, cols = base.shape
     return pl.pallas_call(
         functools.partial(other_kernel, scale, cuts),
         out_shape=[jax.ShapeDtypeStruct((n, b - a, width), F32) for a, b in zip(cuts[:-1], cuts[1:])],
-        in_specs=[SCALAR] + [FULL] * 4,
+        in_specs=[SCALAR, SCALAR] + [FULL] * 4,
         out_specs=[FULL] * (len(cuts) - 1),
         scratch_shapes=[pltpu.VMEM((height, cols), BF16)] * 2,
         compiler_params=params(24),
         cost_estimate=pl.CostEstimate(
             flops=12 * height * cols * cols, bytes_accessed=16 * height * cols, transcendentals=0
         ),
-    )(rows, side, base, lin_h, lin_l)
+    )(at, rows, side, base, lin_h, lin_l)
 
 
 def finish_kernel(cuts, below, *refs):
@@ -242,43 +246,33 @@
     return [lax.all_to_all(piece, axes, split_axis=0, concat_axis=0, tiled=True) for piece in pieces]
 
 
-def weights_of(values, index):
-    slots = jnp.arange(values.shape[0], dtype=jnp.int32)
-    return jnp.sum(jnp.where(index[:, :, None] == slots[None, None, :], values[None, None, :], jnp.float32(0.0)), axis=2)
-
-
 def per_device(amplitudes, interaction, sixj_values, sixj_index, ph_rows, denominators):
     c, height, width = amplitudes.shape
     n_chan, n_z = lax.axis_size("chan"), lax.axis_size("z")
     z, core = lax.axis_index("z"), lax.axis_index("core")
     at = jnp.reshape(z, (1,)).astype(jnp.int32)
-    rows_of = lax.dynamic_slice_in_dim(ph_rows, z, 1)
     scale = 1.0 / (height * width * n_z * 2) ** 0.5
 
     def forward(core):
-        def run(blocks, values, index):
+        def run(blocks, *given):
             parts = exchange(deal(blocks, n_chan, FIRST[core]), "chan")
-            if EARLY1[core]:
-                values = weights_of(values, index)
-            return exchange(mix(values, index, parts, (0, height // n_chan)), CHIPS)[0]
+            mixed, table = mix(given, parts, (0, height // n_chan))
+            return exchange([mixed], CHIPS)[0], table
 
         return run
 
     def backward(core):
-        def run(rows, theirs, values, index, below, *sums):
-            cycle = other(rows, theirs, *sums, scale, THIRD[core])
-            if EARLY[core]:
-                values = weights_of(values, index)
-            back = mix(values, index, exchange(cycle, CHIPS), LAST[core], back=True)
+        def run(at, rows, theirs, table, below, *sums):
+            cycle = other(at, rows, theirs, *sums, scale, THIRD[core])
+            back = mix((table,), exchange(cycle, CHIPS), LAST[core], back=True)
             return finish(exchange(back, "chan"), below, n_chan, LAST[core])
 
         return run
 
-    tables = (sixj_values, sixj_index)
-    mine = lax.cond(core == 0, forward(0), forward(1), amplitudes, *tables)
+    mine, table = lax.cond(core == 0, forward(0), forward(1), amplitudes, sixj_values, sixj_index)
     theirs = lax.ppermute(mine, "core", [(0, 1), (1, 0)])
-    sums = own(at, rows_of, mine, interaction, scale)
-    return lax.cond(core == 0, backward(0), backward(1), rows_of, theirs, *tables, denominators, *sums)
+    sums = own(at, ph_rows, mine, interaction, scale)
+    return lax.cond(core == 0, backward(0), backward(1), at, ph_rows, theirs, table, denominators, *sums)
 
 
 def solution(mesh):

time: 152 us -> 151 us (level)
  blocking collectives: 103 us -> 126 us
  waiting for transfers between devices: 16.1 us -> 0.01 us
  starting transfers between devices: 4.69 us -> 0.01 us
  local copies, waits for them, and re-layouts: 3.14 us -> 1.33 us
    all_to_all x5 -> x6, blocking collectives: 103 us -> 126 us  [exchange(): lax.all_to_all(piece, axes, split_axis=0, concat_axis=0, tiled=True)]
    all_to_all x1 -> x0, waiting for transfers between devices: 16.1 us -> none  [exchange(): lax.all_to_all(piece, axes, split_axis=0, concat_axis=0, tiled=True)]
    all_to_all x1 -> x0, starting transfers between devices: 4.69 us -> none  [exchange(): lax.all_to_all(piece, axes, split_axis=0, concat_axis=0, tiled=True)]
  transfers between devices with their start and end apart: 2 -> 1, of which waited for: 1 -> 0; matrix products, arithmetic and copies ran while one was open for 1% -> 0% of each run, Pallas kernels for 6% -> 7%
where the time goes in v4:
time: 151 us; the launch traced here: 150 us
  blocking collectives  126 us (83%)
  Pallas kernels  23 us (15%)
    all_to_all x6, blocking collectives, exchange(): lax.all_to_all(piece, axes, split_axis=0, concat_axis=0, tiled=True)  126 us
    pallas_call x1, Pallas kernels, own(): pl.pallas_call(functools.partial(own_kernel, scale, block), out_shape=[sd...  10.1 us
    pallas_call x2, Pallas kernels, mix(): pl.pallas_call(functools.partial(mix_kernel, cuts, back), out_shape=shape...  5.35 us
    pallas_call x1, Pallas kernels, other(): pl.pallas_call(functools.partial(other_kernel, scale, cuts), out_shape=[j...  5.3 us
  transfers between devices with their start and end apart: 1, of which 0 were waited for; matrix products, arithmetic and copies ran while one was open for 0% of the time, Pallas kernels for 7%

profile of v4, /device:TPU:1, one launch (start us, length us, event | category | flops | bytes accessed | tf_op | source)
XLA Modules:
  0.0 150.3 jit_solution(8203976603703609861)
XLA Ops:
  0.0 0.0 copy-start.6
  0.0 71.6 %conditional.2 = (f32[64,64,128]{2,1,0:T(8,128)}, f32[64,64]{1,0:T(8,128)S(1)}) conditional(s32[]{:T(128)} %convert_element_type.4, (f32[4,1024,128]{2,1,0:T(8,128)}, f32[64]{0:T(128)}, s32[64,64]{1,0:T(8,128)}) %tuple.19, (f32[4,1024,128]{2,1,0:T(8,128)}, f32[64]{0:T(128)}, s32[64,64]{1,0:T(8,128)}) %tuple.19), branch_computations={%region_0.0_spmd, %region_1.0_spmd} | conditional | flops 1610612736 | bytes 16843848 | solution.py:272
  0.0 1.7 %branch_0_fun.5 = (f32[16,4,8,128]{3,2,1,0:T(8,128)S(1)}, f32[16,4,56,128]{3,2,1,0:T(8,128)S(1)}) custom-call(f32[4,16,64,128]{3,2,1,0:T(8,128)} %bitcast.19), custom_call_target="tpu_custom_call" | custom-call | bytes 4194304 | tf_op jit(solution)/shard_map/cond/branch_0_fun/pallas_call | solution.py:58
  1.7 0.0 copy-start.2
  1.7 0.0 copy-start.4
  1.7 14.9 %all_to_all.40.refs_2_ = f32[64,8,128]{2,1,0:T(8,128)S(1)} all-to-all(f32[64,8,128]{2,1,0:T(8,128)S(1)} %bitcast.16), channel_id=1, replica_groups=mesh['chan'=16,'z'=4,'core'=2] {'chan'}, dimensions={0} | all-to-all | bytes 524288 | tf_op jit(solution)/shard_map/cond/branch_0_fun/all_to_all | solution.py:246
  16.6 20.9 %all_to_all.41.refs_3_ = f32[64,56,128]{2,1,0:T(8,128)S(1)} all-to-all(f32[64,56,128]{2,1,0:T(8,128)S(1)} %bitcast.15), channel_id=1, replica_groups=mesh['chan'=16,'z'=4,'core'=2] {'chan'}, dimensions={0} | all-to-all | bytes 3670016 | tf_op jit(solution)/shard_map/cond/branch_0_fun/all_to_all | solution.py:246
  37.5 0.0 copy-done.2
  37.5 0.0 copy-done.4
  37.5 3.0 %branch_0_fun.6 = (f32[64,64,128]{2,1,0:T(8,128)S(1)}, f32[64,64]{1,0:T(8,128)S(1)}) custom-call(f32[64]{0:T(128)S(1)} %copy-done.4, s32[64,64]{1,0:T(8,128)S(1)} %copy-done.2, f32[64,8,128]{2,1,0:T(8,128)S(1)} %all_to_all.40.refs_2_, f32[64,56,128]{2,1,0:T(8,128)S(1)} %all_to_all.41.refs_3_), custom_call_target="tpu_custom_call" | custom-call | flops 1610612736 | bytes 4194304 | tf_op jit(solution)/shard_map/cond/branch_0_fun/pallas_call | solution.py:115
  40.5 31.1 %all_to_all.42 = f32[64,64,128]{2,1,0:T(8,128)} all-to-all(f32[64,64,128]{2,1,0:T(8,128)S(1)} %get-tuple-element.57), channel_id=1, replica_groups=mesh['chan'=16,'z'=4,'core'=2] {'chan','z'}, dimensions={0} | all-to-all | bytes 4194304 | tf_op jit(solution)/shard_map/cond/branch_0_fun/all_to_all | solution.py:246
  71.6 0.0 collective-permute-start
  71.6 0.0 copy-done.6
  71.6 0.0 copy-start
  71.6 10.1 %shard_map.68 = (f32[1024,512]{1,0:T(8,128)S(1)}, bf16[1024,512]{1,0:T(8,128)(2,1)S(1)}, bf16[1024,512]{1,0:T(8,128)(2,1)S(1)}) custom-call(s32[1]{0:T(128)} %bitcast.11.at, s32[4]{0:T(128)S(1)} %copy-done.6, f32[64,64,128]{2,1,0:T(8,128)} %get-tuple-element.87.side, f32[4,1024,1024]{2,1,0:T(8,128)} %inter.1), custom_call_target="tpu_custom_call" | custom-call | flops 6442450944 | bytes 10485760 | tf_op jit(solution)/shard_map/pallas_call | solution.py:167
  81.7 0.0 collective-permute-done
  81.7 0.0 copy-done
  81.7 67.2 %conditional.3 = (f32[4,1024,128]{2,1,0:T(8,128)S(1)}) conditional(s32[]{:T(128)} %convert_element_type.4, (f32[4,1024,128]{2,1,0:T(8,128)S(1)}, s32[1]{0:T(128)}, s32[4]{0:T(128)S(1)}, f32[64,64,128]{2,1,0:T(8,128)}, f32[1024,512]{1,0:T(8,128)S(1)}, /*index=5*/bf16[1024,512]{1,0:T(8,128)(2,1)S(1)}, bf16[1024,512]{1,0:T(8,128)(2,1)S(1)}, ...), branch_computations={%region_2.0_spmd, %region_3.0_spmd} | conditional | flops 4832362496 | bytes 27262984 | solution.py:275
  81.9 5.3 %branch_0_fun.7 = (f32[64,8,128]{2,1,0:T(8,128)S(1)}, f32[64,56,128]{2,1,0:T(8,128)S(1)}) custom-call(s32[1]{0:T(128)} %get-tuple-element.66.at, s32[4]{0:T(128)S(1)} %get-tuple-element.67.rows, f32[64,64,128]{2,1,0:T(8,128)} %get-tuple-element.68.side, f32[1024,512]{1,0:T(8,128)S(1)} %get-tuple-element.69.base, ...), custom_call_target="tpu_custom_call" | custom-call | flops 3221225472 | bytes 8388608 | tf_op jit(solution)/shard_map/cond/branch_0_fun/pallas_call | solution.py:209
  87.2 15.0 %all_to_all.45.refs_1_ = f32[64,8,128]{2,1,0:T(8,128)S(1)} all-to-all(f32[64,8,128]{2,1,0:T(8,128)S(1)} %get-tuple-element.72), channel_id=1, replica_groups=mesh['chan'=16,'z'=4,'core'=2] {'chan','z'}, dimensions={0} | all-to-all | bytes 524288 | tf_op jit(solution)/shard_map/cond/branch_0_fun/all_to_all | solution.py:246
  102.3 21.8 %all_to_all.46.refs_2_ = f32[64,56,128]{2,1,0:T(8,128)S(1)} all-to-all(f32[64,56,128]{2,1,0:T(8,128)S(1)} %get-tuple-element.73), channel_id=1, replica_groups=mesh['chan'=16,'z'=4,'core'=2] {'chan','z'}, dimensions={0} | all-to-all | bytes 3670016 | tf_op jit(solution)/shard_map/cond/branch_0_fun/all_to_all | solution.py:246
  124.1 2.4 %branch_0_fun.8 = f32[64,64,128]{2,1,0:T(8,128)S(1)} custom-call(f32[64,64]{1,0:T(8,128)S(1)} %get-tuple-element.65.refs_0_, f32[64,8,128]{2,1,0:T(8,128)S(1)} %all_to_all.45.refs_1_, f32[64,56,128]{2,1,0:T(8,128)S(1)} %all_to_all.46.refs_2_), custom_call_target="tpu_custom_call" | custom-call | flops 1610612736 | bytes 4194304 | tf_op jit(solution)/shard_map/cond/branch_0_fun/pallas_call | solution.py:115
  126.5 21.8 %all_to_all.47 = f32[64,64,128]{2,1,0:T(8,128)S(1)} all-to-all(f32[64,64,128]{2,1,0:T(8,128)S(1)} %branch_0_fun.8), channel_id=1, replica_groups=mesh['chan'=16,'z'=4,'core'=2] {'chan'}, dimensions={0} | all-to-all | bytes 4194304 | tf_op jit(solution)/shard_map/cond/branch_0_fun/all_to_all | solution.py:246
  148.2 0.5 branch_0_fun.9
  149.0 0.0 copy-start.1
  149.0 1.3 copy-done.1
Async XLA Ops:
  0.0 71.6 %copy-start.6 = (s32[4]{0:T(128)S(1)}, s32[4]{0:T(128)}, u32[]{:S(2)}) copy-start(s32[4]{0:T(128)} %rows.1) | copy-start | bytes 52
  1.7 35.8 %copy-start.2 = (s32[64,64]{1,0:T(8,128)S(1)}, s32[64,64]{1,0:T(8,128)}, u32[]{:S(2)}) copy-start(s32[64,64]{1,0:T(8,128)} %get-tuple-element.53.refs_1_) | copy-start | bytes 49156 | tf_op jit(solution)/shard_map/cond
  1.7 35.8 %copy-start.4 = (f32[64]{0:T(128)S(1)}, f32[64]{0:T(128)}, u32[]{:S(2)}) copy-start(f32[64]{0:T(128)} %get-tuple-element.52.refs_0_) | copy-start | bytes 772 | tf_op jit(solution)/shard_map/cond
  71.6 10.1 %collective-permute-start = (f32[64,64,128]{2,1,0:T(8,128)}, f32[64,64,128]{2,1,0:T(8,128)}, u32[]{:S(2)}, u32[]{:S(2)}) collective-permute-start(f32[64,64,128]{2,1,0:T(8,128)} %get-tuple-element.87.side), channel_id=1, source_target_pairs={{0,1},{1,0},{2,3},{3,2},{4,5},{5,4},{6,7},{7,6},{8,9},{9,8},{10,11... | collective-permute-start | bytes 6291464 | tf_op jit(solution)/shard_map/ppermute | solution.py:273
  71.6 10.1 %copy-start = (f32[4,1024,128]{2,1,0:T(8,128)S(1)}, f32[4,1024,128]{2,1,0:T(8,128)}, u32[]{:S(2)}) copy-start(f32[4,1024,128]{2,1,0:T(8,128)} %param.15) | copy-start | bytes 6291460
  149.0 1.3 copy-start.1

commit v5 on v4

--- a/solution.py
+++ b/solution.py
@@ -10,7 +10,6 @@
 CHIPS = ("chan", "z")
 FIRST = ((0, 64), (0, 8, 64))
 THIRD = ((0, 64), (0, 8, 64))
-OWN_MIB = 52
 LAST = ((0, 64), (0, 64))
 MIB = 2**20
 BF16, F32 = jnp.bfloat16, jnp.float32
@@ -136,18 +135,15 @@
             scratch_low[span, k * width : (k + 1) * width] = low
 
 
-def own_kernel(scale, block, at, rows, side, inter, acc, lin_h, lin_l, v, raw, side_h, side_l, sem):
+def own_kernel(scale, block, at, rows, side, inter, acc, lin_h, lin_l, v, side_h, side_l, sem):
     height = v.shape[0]
-    first = pltpu.make_async_copy(side, raw, sem.at[0])
-    first.start()
     copies = [
-        pltpu.make_async_copy(inter.at[at[0], pl.ds(r, block)], v.at[pl.ds(r, block)], sem.at[1 + r // block])
+        pltpu.make_async_copy(inter.at[at[0], pl.ds(r, block)], v.at[pl.ds(r, block)], sem.at[r // block])
         for r in range(0, height, block)
     ]
     for copy in copies:
         copy.start()
-    first.wait()
-    gather_side(raw, rows[at[0]], side_h, side_l)
+    gather_side(side, rows[at[0]], side_h, side_l)
     mine = (side_h[...], side_l[...])
     for r, copy in zip(range(0, height, block), copies):
         copy.wait()
@@ -167,20 +163,24 @@
     return pl.pallas_call(
         functools.partial(own_kernel, scale, block),
         out_shape=[sds((height, cols), F32), sds((height, cols), BF16), sds((height, cols), BF16)],
-        in_specs=[SCALAR, SCALAR, ANY, ANY],
+        in_specs=[SCALAR, SCALAR, FULL, ANY],
         out_specs=[FULL] * 3,
         scratch_shapes=[
             pltpu.VMEM((height, height), F32),
-            pltpu.VMEM(side.shape, F32),
             pltpu.VMEM((height, cols), BF16),
             pltpu.VMEM((height, cols), BF16),
-            pltpu.SemaphoreType.DMA((1 + height // block,)),
+            pltpu.SemaphoreType.DMA((height // block,)),
         ],
-        compiler_params=params(OWN_MIB),
+        compiler_params=params(24),
         cost_estimate=pl.CostEstimate(
             flops=12 * height * height * cols, bytes_accessed=4 * height * (height + 3 * cols), transcendentals=0
         ),
-    )(at, rows, side, inter)
+    )(
+        at,
+        rows,
+        pltpu.with_memory_space_constraint(side, pltpu.VMEM),
+        pltpu.with_memory_space_constraint(inter, pltpu.HBM),
+    )
 
 
 def other_kernel(scale, cuts, at, rows, side, base, lin_h, lin_l, *refs):
@@ -216,7 +216,7 @@
         cost_estimate=pl.CostEstimate(
             flops=12 * height * cols * cols, bytes_accessed=16 * height * cols, transcendentals=0
         ),
-    )(at, rows, side, base, lin_h, lin_l)
+    )(at, rows, pltpu.with_memory_space_constraint(side, pltpu.VMEM), base, lin_h, lin_l)
 
 
 def finish_kernel(cuts, below, *refs):

time: 151 us -> 150 us (level)
  transfers between devices with their start and end apart: 1 -> 1, of which waited for: 0 -> 0; matrix products, arithmetic and copies ran while one was open for 0% -> 0% of each run, Pallas kernels for 7% -> 6%
where the time goes in v5:
time: 150 us; the launch traced here: 149 us
  blocking collectives  125 us (83%)
  Pallas kernels  22 us (15%)
    all_to_all x6, blocking collectives, exchange(): lax.all_to_all(piece, axes, split_axis=0, concat_axis=0, tiled=True)  125 us
    pallas_call x1, Pallas kernels, own(): pl.pallas_call(functools.partial(own_kernel, scale, block), out_shape=[sd...  9.19 us
    pallas_call x2, Pallas kernels, mix(): pl.pallas_call(functools.partial(mix_kernel, cuts, back), out_shape=shape...  5.35 us
    pallas_call x1, Pallas kernels, other(): pl.pallas_call(functools.partial(other_kernel, scale, cuts), out_shape=[j...  5.29 us
  transfers between devices with their start and end apart: 1, of which 0 were waited for; matrix products, arithmetic and copies ran while one was open for 0% of the time, Pallas kernels for 6%

profile of v5, /device:TPU:1, one launch (start us, length us, event | category | flops | bytes accessed | tf_op | source)
XLA Modules:
  0.0 149.3 jit_solution(6913234468708276571)
XLA Ops:
  0.0 0.0 copy-start.6
  0.0 71.5 %conditional.2 = (f32[64,64,128]{2,1,0:T(8,128)S(1)}, f32[64,64]{1,0:T(8,128)S(1)}) conditional(s32[]{:T(128)} %convert_element_type.4, (f32[4,1024,128]{2,1,0:T(8,128)}, f32[64]{0:T(128)}, s32[64,64]{1,0:T(8,128)}) %tuple.19, (f32[4,1024,128]{2,1,0:T(8,128)}, f32[64]{0:T(128)}, s32[64,64]{1,0:T(8,128)}) %tuple.19), branch_computations={%region_0.0_spmd, %region_1.0_spmd} | conditional | flops 1610612736 | bytes 16843848 | solution.py:272
  0.0 1.7 %branch_0_fun.5 = (f32[16,4,8,128]{3,2,1,0:T(8,128)S(1)}, f32[16,4,56,128]{3,2,1,0:T(8,128)S(1)}) custom-call(f32[4,16,64,128]{3,2,1,0:T(8,128)} %bitcast.19), custom_call_target="tpu_custom_call" | custom-call | bytes 4194304 | tf_op jit(solution)/shard_map/cond/branch_0_fun/pallas_call | solution.py:57
  1.7 0.0 copy-start.2
  1.7 0.0 copy-start.4
  1.7 14.9 %all_to_all.40.refs_2_ = f32[64,8,128]{2,1,0:T(8,128)S(1)} all-to-all(f32[64,8,128]{2,1,0:T(8,128)S(1)} %bitcast.16), channel_id=1, replica_groups=mesh['chan'=16,'z'=4,'core'=2] {'chan'}, dimensions={0} | all-to-all | bytes 524288 | tf_op jit(solution)/shard_map/cond/branch_0_fun/all_to_all | solution.py:246
  16.6 20.9 %all_to_all.41.refs_3_ = f32[64,56,128]{2,1,0:T(8,128)S(1)} all-to-all(f32[64,56,128]{2,1,0:T(8,128)S(1)} %bitcast.15), channel_id=1, replica_groups=mesh['chan'=16,'z'=4,'core'=2] {'chan'}, dimensions={0} | all-to-all | bytes 3670016 | tf_op jit(solution)/shard_map/cond/branch_0_fun/all_to_all | solution.py:246
  37.5 0.0 copy-done.2
  37.5 0.0 copy-done.4
  37.5 3.0 %branch_0_fun.6 = (f32[64,64,128]{2,1,0:T(8,128)S(1)}, f32[64,64]{1,0:T(8,128)S(1)}) custom-call(f32[64]{0:T(128)S(1)} %copy-done.4, s32[64,64]{1,0:T(8,128)S(1)} %copy-done.2, f32[64,8,128]{2,1,0:T(8,128)S(1)} %all_to_all.40.refs_2_, f32[64,56,128]{2,1,0:T(8,128)S(1)} %all_to_all.41.refs_3_), custom_call_target="tpu_custom_call" | custom-call | flops 1610612736 | bytes 4194304 | tf_op jit(solution)/shard_map/cond/branch_0_fun/pallas_call | solution.py:114
  40.5 31.0 %all_to_all.42 = f32[64,64,128]{2,1,0:T(8,128)S(1)} all-to-all(f32[64,64,128]{2,1,0:T(8,128)S(1)} %get-tuple-element.57), channel_id=1, replica_groups=mesh['chan'=16,'z'=4,'core'=2] {'chan','z'}, dimensions={0} | all-to-all | bytes 4194304 | tf_op jit(solution)/shard_map/cond/branch_0_fun/all_to_all | solution.py:246
  71.5 0.0 collective-permute-start
  71.5 0.0 copy-done.6
  71.5 0.0 copy-start
  71.5 9.2 %shard_map.68 = (f32[1024,512]{1,0:T(8,128)S(1)}, bf16[1024,512]{1,0:T(8,128)(2,1)S(1)}, bf16[1024,512]{1,0:T(8,128)(2,1)S(1)}) custom-call(s32[1]{0:T(128)} %bitcast.11.at, s32[4]{0:T(128)S(1)} %copy-done.6, f32[64,64,128]{2,1,0:T(8,128)S(1)} %get-tuple-element.87.side, f32[4,1024,1024]{2,1,0:T(8,128)} %inter.1), custom_call_target="tpu_custom_call" | custom-call | flops 6442450944 | bytes 10485760 | tf_op jit(solution)/shard_map/pallas_call | solution.py:163
  80.7 0.0 collective-permute-done
  80.7 0.0 copy-done
  80.7 67.2 %conditional.3 = (f32[4,1024,128]{2,1,0:T(8,128)S(1)}) conditional(s32[]{:T(128)} %convert_element_type.4, (f32[4,1024,128]{2,1,0:T(8,128)S(1)}, s32[1]{0:T(128)}, s32[4]{0:T(128)S(1)}, f32[64,64,128]{2,1,0:T(8,128)}, f32[1024,512]{1,0:T(8,128)S(1)}, /*index=5*/bf16[1024,512]{1,0:T(8,128)(2,1)S(1)}, bf16[1024,512]{1,0:T(8,128)(2,1)S(1)}, ...), branch_computations={%region_2.0_spmd, %region_3.0_spmd} | conditional | flops 4832362496 | bytes 27262984 | solution.py:275
  80.9 5.3 %branch_0_fun.7 = (f32[64,8,128]{2,1,0:T(8,128)S(1)}, f32[64,56,128]{2,1,0:T(8,128)S(1)}) custom-call(s32[1]{0:T(128)} %get-tuple-element.66.at, s32[4]{0:T(128)S(1)} %get-tuple-element.67.rows, f32[64,64,128]{2,1,0:T(8,128)} %get-tuple-element.68.side, f32[1024,512]{1,0:T(8,128)S(1)} %get-tuple-element.69.base, ...), custom_call_target="tpu_custom_call" | custom-call | flops 3221225472 | bytes 8388608 | tf_op jit(solution)/shard_map/cond/branch_0_fun/pallas_call | solution.py:209
  86.2 15.1 %all_to_all.45.refs_1_ = f32[64,8,128]{2,1,0:T(8,128)S(1)} all-to-all(f32[64,8,128]{2,1,0:T(8,128)S(1)} %get-tuple-element.72), channel_id=1, replica_groups=mesh['chan'=16,'z'=4,'core'=2] {'chan','z'}, dimensions={0} | all-to-all | bytes 524288 | tf_op jit(solution)/shard_map/cond/branch_0_fun/all_to_all | solution.py:246
  101.3 21.8 %all_to_all.46.refs_2_ = f32[64,56,128]{2,1,0:T(8,128)S(1)} all-to-all(f32[64,56,128]{2,1,0:T(8,128)S(1)} %get-tuple-element.73), channel_id=1, replica_groups=mesh['chan'=16,'z'=4,'core'=2] {'chan','z'}, dimensions={0} | all-to-all | bytes 3670016 | tf_op jit(solution)/shard_map/cond/branch_0_fun/all_to_all | solution.py:246
  123.1 2.4 %branch_0_fun.8 = f32[64,64,128]{2,1,0:T(8,128)S(1)} custom-call(f32[64,64]{1,0:T(8,128)S(1)} %get-tuple-element.65.refs_0_, f32[64,8,128]{2,1,0:T(8,128)S(1)} %all_to_all.45.refs_1_, f32[64,56,128]{2,1,0:T(8,128)S(1)} %all_to_all.46.refs_2_), custom_call_target="tpu_custom_call" | custom-call | flops 1610612736 | bytes 4194304 | tf_op jit(solution)/shard_map/cond/branch_0_fun/pallas_call | solution.py:114
  125.4 21.8 %all_to_all.47 = f32[64,64,128]{2,1,0:T(8,128)S(1)} all-to-all(f32[64,64,128]{2,1,0:T(8,128)S(1)} %branch_0_fun.8), channel_id=1, replica_groups=mesh['chan'=16,'z'=4,'core'=2] {'chan'}, dimensions={0} | all-to-all | bytes 4194304 | tf_op jit(solution)/shard_map/cond/branch_0_fun/all_to_all | solution.py:246
  147.2 0.5 branch_0_fun.9
  148.0 0.0 copy-start.1
  148.0 1.3 copy-done.1
Async XLA Ops:
  0.0 71.5 %copy-start.6 = (s32[4]{0:T(128)S(1)}, s32[4]{0:T(128)}, u32[]{:S(2)}) copy-start(s32[4]{0:T(128)} %rows.1) | copy-start | bytes 52
  1.7 35.8 %copy-start.2 = (s32[64,64]{1,0:T(8,128)S(1)}, s32[64,64]{1,0:T(8,128)}, u32[]{:S(2)}) copy-start(s32[64,64]{1,0:T(8,128)} %get-tuple-element.53.refs_1_) | copy-start | bytes 49156 | tf_op jit(solution)/shard_map/cond
  1.7 35.8 %copy-start.4 = (f32[64]{0:T(128)S(1)}, f32[64]{0:T(128)}, u32[]{:S(2)}) copy-start(f32[64]{0:T(128)} %get-tuple-element.52.refs_0_) | copy-start | bytes 772 | tf_op jit(solution)/shard_map/cond
  71.5 9.2 %collective-permute-start = (f32[64,64,128]{2,1,0:T(8,128)S(1)}, f32[64,64,128]{2,1,0:T(8,128)}, u32[]{:S(2)}, u32[]{:S(2)}) collective-permute-start(f32[64,64,128]{2,1,0:T(8,128)S(1)} %get-tuple-element.87.side), channel_id=1, source_target_pairs={{0,1},{1,0},{2,3},{3,2},{4,5},{5,4},{6,7},{7,6},{8,9},{9,8},{10,11... | collective-permute-start | bytes 6291464 | tf_op jit(solution)/shard_map/ppermute | solution.py:273
  71.5 9.2 %copy-start = (f32[4,1024,128]{2,1,0:T(8,128)S(1)}, f32[4,1024,128]{2,1,0:T(8,128)}, u32[]{:S(2)}) copy-start(f32[4,1024,128]{2,1,0:T(8,128)} %param.15) | copy-start | bytes 6291460
  148.0 1.3 copy-start.1

commit v6 on v5

--- a/solution.py
+++ b/solution.py
@@ -33,37 +33,6 @@
 
 def params(mib):
     return pltpu.CompilerParams(vmem_limit_bytes=mib * MIB)
-
-
-def deal_kernel(cuts, blocks, *refs):
-    outs, sems = refs[:-1], refs[-1]
-    copies = [
-        pltpu.make_async_copy(
-            blocks.at[c, :, pl.ds(cuts[k], cuts[k + 1] - cuts[k])], out.at[:, c], sems.at[k * blocks.shape[0] + c]
-        )
-        for k, out in enumerate(outs)
-        for c in range(blocks.shape[0])
-    ]
-    for copy in copies:
-        copy.start()
-    for copy in copies:
-        copy.wait()
-
-
-def deal(blocks, n, cuts):
-    c, height, width = blocks.shape
-    part = height // n
-    sizes = [b - a for a, b in zip(cuts[:-1], cuts[1:])]
-    pieces = pl.pallas_call(
-        functools.partial(deal_kernel, cuts),
-        out_shape=[jax.ShapeDtypeStruct((n, c, rows, width), F32) for rows in sizes],
-        in_specs=[ANY],
-        out_specs=[FULL] * len(sizes),
-        scratch_shapes=[pltpu.SemaphoreType.DMA((len(sizes) * c,))],
-        compiler_params=params(8),
-        cost_estimate=pl.CostEstimate(flops=0, bytes_accessed=8 * c * height * width, transcendentals=0),
-    )(blocks.reshape(c, n, part, width))
-    return [piece.reshape(n * c, rows, width) for piece, rows in zip(pieces, sizes)]
 
 
 def spread_table(table):
@@ -80,19 +49,60 @@
     return tuple(spread)
 
 
-def mix_kernel(cuts, back, *refs):
-    n_in, n_out = (1, len(cuts) - 1) if back else (2, len(cuts))
+def deal_kernel(cuts, blocks, values, index, *refs):
+    n_out = len(cuts) - 1
+    outs, (table, spread_h, spread_l, slots, known, sems) = refs[:n_out], refs[n_out:]
+    c = blocks.shape[0]
+    copies = [
+        pltpu.make_async_copy(blocks.at[i, :, pl.ds(cuts[k], cuts[k + 1] - cuts[k])], out.at[:, i], sems.at[k * c + i])
+        for k, out in enumerate(outs)
+        for i in range(c)
+    ]
+    small = [
+        pltpu.make_async_copy(index, slots, sems.at[n_out * c]),
+        pltpu.make_async_copy(values, known, sems.at[n_out * c + 1]),
+    ]
+    for copy in small + copies:
+        copy.start()
+    for copy in small:
+        copy.wait()
+    made = jnp.zeros(index.shape, F32)
+    for slot in range(values.shape[0]):
+        made = jnp.where(slots[...] == slot, known[slot], made)
+    table[...] = made
+    spread_h[...], spread_l[...] = spread_table(made)
+    for copy in copies:
+        copy.wait()
+
+
+def deal(blocks, values, index, n, cuts):
+    c, height, width = blocks.shape
+    part = height // n
+    sizes = [b - a for a, b in zip(cuts[:-1], cuts[1:])]
+    wide = index.shape[0] * SUB
+    sds = jax.ShapeDtypeStruct
+    *pieces, table, spread_h, spread_l = pl.pallas_call(
+        functools.partial(deal_kernel, cuts),
+        out_shape=[sds((n, c, rows, width), F32) for rows in sizes]
+        + [sds(index.shape, F32), sds((wide, wide), BF16), sds((wide, wide), BF16)],
+        in_specs=[ANY] * 3,
+        out_specs=[FULL] * (len(sizes) + 3),
+        scratch_shapes=[
+            pltpu.VMEM(index.shape, jnp.int32),
+            pltpu.SMEM(values.shape, F32),
+            pltpu.SemaphoreType.DMA((len(sizes) * c + 2,)),
+        ],
+        compiler_params=params(12),
+        cost_estimate=pl.CostEstimate(flops=0, bytes_accessed=8 * c * height * width, transcendentals=0),
+    )(blocks.reshape(c, n, part, width), values, index)
+    return [piece.reshape(n * c, rows, width) for piece, rows in zip(pieces, sizes)], table, (spread_h, spread_l)
+
+
+def mix_kernel(cuts, n_in, *refs):
+    n_out = len(cuts) - 1
     given, pieces, outs = refs[:n_in], refs[n_in:-n_out], refs[-n_out:]
     n, _, width = outs[0].shape
-    if back:
-        table = given[0][...].T
-    else:
-        values, index = given
-        table = jnp.zeros(index.shape, F32)
-        for slot in range(values.shape[0]):
-            table = jnp.where(index[...] == slot, values[slot], table)
-        outs[-1][...] = table
-    spread = spread_table(table)
+    spread = spread_table(given[0][...].T) if n_in == 1 else tuple(ref[...] for ref in given)
     groups = [(ref, row) for ref in pieces for row in range(0, ref.shape[1], SUB)]
     for at in range(0, len(groups), 2):
         x = jnp.concatenate(
@@ -105,17 +115,14 @@
             outs[i][:, row - cuts[i] : row - cuts[i] + SUB, :] = y[:, k * width : (k + 1) * width].reshape(n, SUB, width)
 
 
-def mix(given, pieces, cuts, back=False):
+def mix(given, pieces, cuts):
     n, _, width = pieces[0].shape
     part = cuts[-1]
-    shapes = [jax.ShapeDtypeStruct((n, b - a, width), F32) for a, b in zip(cuts[:-1], cuts[1:])]
-    if not back:
-        shapes.append(jax.ShapeDtypeStruct((n, n), F32))
-    return pl.pallas_call(
-        functools.partial(mix_kernel, cuts, back),
-        out_shape=shapes,
-        in_specs=([FULL] if back else [SCALAR, FULL]) + [FULL] * len(pieces),
-        out_specs=[FULL] * len(shapes),
+    return pl.pallas_call(
+        functools.partial(mix_kernel, cuts, len(given)),
+        out_shape=[jax.ShapeDtypeStruct((n, b - a, width), F32) for a, b in zip(cuts[:-1], cuts[1:])],
+        in_specs=[FULL] * (len(given) + len(pieces)),
+        out_specs=[FULL] * (len(cuts) - 1),
         compiler_params=params(16),
         cost_estimate=pl.CostEstimate(
             flops=6 * n * n * part * width * SUB, bytes_accessed=8 * n * part * width, transcendentals=0
@@ -254,17 +261,17 @@
     scale = 1.0 / (height * width * n_z * 2) ** 0.5
 
     def forward(core):
-        def run(blocks, *given):
-            parts = exchange(deal(blocks, n_chan, FIRST[core]), "chan")
-            mixed, table = mix(given, parts, (0, height // n_chan))
-            return exchange([mixed], CHIPS)[0], table
+        def run(blocks, values, index):
+            pieces, table, spread = deal(blocks, values, index, n_chan, FIRST[core])
+            mixed = mix(spread, exchange(pieces, "chan"), (0, height // n_chan))
+            return exchange(mixed, CHIPS)[0], table
 
         return run
 
     def backward(core):
         def run(at, rows, theirs, table, below, *sums):
             cycle = other(at, rows, theirs, *sums, scale, THIRD[core])
-            back = mix((table,), exchange(cycle, CHIPS), LAST[core], back=True)
+            back = mix((table,), exchange(cycle, CHIPS), LAST[core])
             return finish(exchange(back, "chan"), below, n_chan, LAST[core])
 
         return run

time: 150 us -> 148 us (0.987)
  no operation moved by 1% of the time
where the time goes in v6:
time: 148 us
  blocking collectives  125 us (84%)
  Pallas kernels  20.9 us (14%)
    all_to_all x6, blocking collectives, exchange(): lax.all_to_all(piece, axes, split_axis=0, concat_axis=0, tiled=True)  125 us
    pallas_call x1, Pallas kernels, own(): pl.pallas_call(functools.partial(own_kernel, scale, block), out_shape=[sd...  9.19 us
    pallas_call x1, Pallas kernels, other(): pl.pallas_call(functools.partial(other_kernel, scale, cuts), out_shape=[j...  5.31 us
    pallas_call x2, Pallas kernels, mix(): pl.pallas_call(functools.partial(mix_kernel, cuts, len(given)), out_shape...  4.17 us
  transfers between devices with their start and end apart: 1, of which 0 were waited for; matrix products, arithmetic and copies ran while one was open for 0% of the time, Pallas kernels for 6%

profile of v6, /device:TPU:1, one launch (start us, length us, event | category | flops | bytes accessed | tf_op | source)
XLA Modules:
  0.0 147.8 jit_solution(8911456403366870129)
XLA Ops:
  0.0 0.0 copy-start.2
  0.0 70.4 %conditional.2 = (f32[64,64,128]{2,1,0:T(8,128)S(1)}, f32[64,64]{1,0:T(8,128)S(1)}) conditional(s32[]{:T(128)} %convert_element_type.4, (f32[4,1024,128]{2,1,0:T(8,128)}, f32[64]{0:T(128)}, s32[64,64]{1,0:T(8,128)}) %tuple.19, (f32[4,1024,128]{2,1,0:T(8,128)}, f32[64]{0:T(128)}, s32[64,64]{1,0:T(8,128)}) %tuple.19), branch_computations={%region_0.0_spmd, %region_1.0_spmd} | conditional | flops 1610612736 | bytes 16777232 | solution.py:279
  0.0 1.7 %branch_0_fun.5 = (f32[16,4,8,128]{3,2,1,0:T(8,128)S(1)}, f32[16,4,56,128]{3,2,1,0:T(8,128)S(1)}, f32[64,64]{1,0:T(8,128)S(1)}, bf16[512,512]{1,0:T(8,128)(2,1)S(1)}, bf16[512,512]{1,0:T(8,128)(2,1)S(1)}) custom-call(f32[4,16,64,128]{3,2,1,0:T(8,128)} %bitcast.19, f32[64]{0:T(128)} %get-tuple-element.53.values, s32[64,64]{1,0:T(8,128)} %get-tuple-element.54.index), custom_call_target="tpu_custom_call" | custom-call | bytes 4194304 | tf_op jit(solution)/shard_map/cond/branch_0_fun/pallas_call | solution.py:84
  1.7 14.9 %all_to_all.40.refs_2_ = f32[64,8,128]{2,1,0:T(8,128)S(1)} all-to-all(f32[64,8,128]{2,1,0:T(8,128)S(1)} %bitcast.16), channel_id=1, replica_groups=mesh['chan'=16,'z'=4,'core'=2] {'chan'}, dimensions={0} | all-to-all | bytes 524288 | tf_op jit(solution)/shard_map/cond/branch_0_fun/all_to_all | solution.py:253
  16.6 20.9 %all_to_all.41.refs_3_ = f32[64,56,128]{2,1,0:T(8,128)S(1)} all-to-all(f32[64,56,128]{2,1,0:T(8,128)S(1)} %bitcast.15), channel_id=1, replica_groups=mesh['chan'=16,'z'=4,'core'=2] {'chan'}, dimensions={0} | all-to-all | bytes 3670016 | tf_op jit(solution)/shard_map/cond/branch_0_fun/all_to_all | solution.py:253
  37.5 1.8 %branch_0_fun.6 = f32[64,64,128]{2,1,0:T(8,128)S(1)} custom-call(bf16[512,512]{1,0:T(8,128)(2,1)S(1)} %get-tuple-element.55.refs_0_, bf16[512,512]{1,0:T(8,128)(2,1)S(1)} %get-tuple-element.56.refs_1_, f32[64,8,128]{2,1,0:T(8,128)S(1)} %all_to_all.40.refs_2_, f32[64,56,128]{2,1,0:T(8,128)S(1)} %all_to_all.41.refs_3_), custom_call_target="tpu_custom_call" | custom-call | flops 1610612736 | bytes 4194304 | tf_op jit(solution)/shard_map/cond/branch_0_fun/pallas_call | solution.py:121
  39.3 31.0 %all_to_all.42 = f32[64,64,128]{2,1,0:T(8,128)S(1)} all-to-all(f32[64,64,128]{2,1,0:T(8,128)S(1)} %branch_0_fun.6), channel_id=1, replica_groups=mesh['chan'=16,'z'=4,'core'=2] {'chan','z'}, dimensions={0} | all-to-all | bytes 4194304 | tf_op jit(solution)/shard_map/cond/branch_0_fun/all_to_all | solution.py:253
  70.4 0.0 collective-permute-start
  70.4 0.0 copy-done.2
  70.4 0.0 copy-start
  70.4 9.2 %shard_map.68 = (f32[1024,512]{1,0:T(8,128)S(1)}, bf16[1024,512]{1,0:T(8,128)(2,1)S(1)}, bf16[1024,512]{1,0:T(8,128)(2,1)S(1)}) custom-call(s32[1]{0:T(128)} %bitcast.11.at, s32[4]{0:T(128)S(1)} %copy-done.2, f32[64,64,128]{2,1,0:T(8,128)S(1)} %get-tuple-element.90.side, f32[4,1024,1024]{2,1,0:T(8,128)} %inter.1), custom_call_target="tpu_custom_call" | custom-call | flops 6442450944 | bytes 10485760 | tf_op jit(solution)/shard_map/pallas_call | solution.py:170
  79.6 0.0 collective-permute-done
  79.6 0.0 copy-done
  79.6 66.9 %conditional.3 = (f32[4,1024,128]{2,1,0:T(8,128)S(1)}) conditional(s32[]{:T(128)} %convert_element_type.4, (f32[4,1024,128]{2,1,0:T(8,128)S(1)}, s32[1]{0:T(128)}, s32[4]{0:T(128)S(1)}, f32[64,64,128]{2,1,0:T(8,128)}, f32[1024,512]{1,0:T(8,128)S(1)}, /*index=5*/bf16[1024,512]{1,0:T(8,128)(2,1)S(1)}, bf16[1024,512]{1,0:T(8,128)(2,1)S(1)}, ...), branch_computations={%region_2.0_spmd, %region_3.0_spmd} | conditional | flops 4832362496 | bytes 27262984 | solution.py:282
  79.6 5.3 %branch_0_fun.7 = (f32[64,8,128]{2,1,0:T(8,128)S(1)}, f32[64,56,128]{2,1,0:T(8,128)S(1)}) custom-call(s32[1]{0:T(128)} %get-tuple-element.69.at, s32[4]{0:T(128)S(1)} %get-tuple-element.70.rows, f32[64,64,128]{2,1,0:T(8,128)} %get-tuple-element.71.side, f32[1024,512]{1,0:T(8,128)S(1)} %get-tuple-element.72.base, ...), custom_call_target="tpu_custom_call" | custom-call | flops 3221225472 | bytes 8388608 | tf_op jit(solution)/shard_map/cond/branch_0_fun/pallas_call | solution.py:216
  84.9 15.1 %all_to_all.45.refs_1_ = f32[64,8,128]{2,1,0:T(8,128)S(1)} all-to-all(f32[64,8,128]{2,1,0:T(8,128)S(1)} %get-tuple-element.75), channel_id=1, replica_groups=mesh['chan'=16,'z'=4,'core'=2] {'chan','z'}, dimensions={0} | all-to-all | bytes 524288 | tf_op jit(solution)/shard_map/cond/branch_0_fun/all_to_all | solution.py:253
  100.0 21.7 %all_to_all.46.refs_2_ = f32[64,56,128]{2,1,0:T(8,128)S(1)} all-to-all(f32[64,56,128]{2,1,0:T(8,128)S(1)} %get-tuple-element.76), channel_id=1, replica_groups=mesh['chan'=16,'z'=4,'core'=2] {'chan','z'}, dimensions={0} | all-to-all | bytes 3670016 | tf_op jit(solution)/shard_map/cond/branch_0_fun/all_to_all | solution.py:253
  121.7 2.4 %branch_0_fun.8 = f32[64,64,128]{2,1,0:T(8,128)S(1)} custom-call(f32[64,64]{1,0:T(8,128)S(1)} %get-tuple-element.68.refs_0_, f32[64,8,128]{2,1,0:T(8,128)S(1)} %all_to_all.45.refs_1_, f32[64,56,128]{2,1,0:T(8,128)S(1)} %all_to_all.46.refs_2_), custom_call_target="tpu_custom_call" | custom-call | flops 1610612736 | bytes 4194304 | tf_op jit(solution)/shard_map/cond/branch_0_fun/pallas_call | solution.py:121
  124.1 21.9 %all_to_all.47 = f32[64,64,128]{2,1,0:T(8,128)S(1)} all-to-all(f32[64,64,128]{2,1,0:T(8,128)S(1)} %branch_0_fun.8), channel_id=1, replica_groups=mesh['chan'=16,'z'=4,'core'=2] {'chan'}, dimensions={0} | all-to-all | bytes 4194304 | tf_op jit(solution)/shard_map/cond/branch_0_fun/all_to_all | solution.py:253
  145.9 0.5 branch_0_fun.9
  146.5 0.0 copy-start.1
  146.5 1.3 copy-done.1
Async XLA Ops:
  0.0 70.4 %copy-start.2 = (s32[4]{0:T(128)S(1)}, s32[4]{0:T(128)}, u32[]{:S(2)}) copy-start(s32[4]{0:T(128)} %rows.1) | copy-start | bytes 52
  70.4 9.2 %collective-permute-start = (f32[64,64,128]{2,1,0:T(8,128)S(1)}, f32[64,64,128]{2,1,0:T(8,128)}, u32[]{:S(2)}, u32[]{:S(2)}) collective-permute-start(f32[64,64,128]{2,1,0:T(8,128)S(1)} %get-tuple-element.90.side), channel_id=1, source_target_pairs={{0,1},{1,0},{2,3},{3,2},{4,5},{5,4},{6,7},{7,6},{8,9},{9,8},{10,11... | collective-permute-start | bytes 6291464 | tf_op jit(solution)/shard_map/ppermute | solution.py:280
  70.4 9.2 %copy-start = (f32[4,1024,128]{2,1,0:T(8,128)S(1)}, f32[4,1024,128]{2,1,0:T(8,128)}, u32[]{:S(2)}) copy-start(f32[4,1024,128]{2,1,0:T(8,128)} %param.15) | copy-start | bytes 6291460
  146.5 1.3 copy-start.1

commit v7 on v6

--- a/solution.py
+++ b/solution.py
@@ -8,7 +8,7 @@
 from jax.sharding import Mesh, PartitionSpec as P
 
 CHIPS = ("chan", "z")
-FIRST = ((0, 64), (0, 8, 64))
+FIRST = ((0, 64), (0, 16, 64))
 THIRD = ((0, 64), (0, 8, 64))
 LAST = ((0, 64), (0, 64))
 MIB = 2**20
@@ -190,11 +190,16 @@
     )
 
 
-def other_kernel(scale, cuts, at, rows, side, base, lin_h, lin_l, *refs):
-    outs, (side_h, side_l) = refs[:-2], refs[-2:]
+def other_kernel(scale, cuts, at, rows, table, side, base, lin_h, lin_l, *refs):
+    outs, spreads, (raw, side_h, side_l, sem) = refs[:-6], refs[-6:-4], refs[-4:]
+    arriving = pltpu.make_async_copy(side, raw, sem.at[0])
+    arriving.start()
+    for ref, value in zip(spreads, spread_table(table[...].T)):
+        ref[...] = value
+    arriving.wait()
     n, part, width = side.shape
     n_z = side_h.shape[1] // width
-    gather_side(side, rows[at[0]], side_h, side_l)
+    gather_side(raw, rows[at[0]], side_h, side_l)
     theirs = (side_h[...], side_l[...])
     inner = halves(dot3(theirs, (lin_h[...], lin_l[...]), ((0,), (0,))) * scale)
     step = 4
@@ -210,43 +215,54 @@
                     out[(g0 + g) * n_z + k] = tile[cuts[i] : cuts[i + 1]]
 
 
-def other(at, rows, side, base, lin_h, lin_l, scale, cuts):
+def other(at, rows, table, side, base, lin_h, lin_l, scale, cuts):
     n, part, width = side.shape
     height, cols = base.shape
-    return pl.pallas_call(
+    wide = table.shape[0] * SUB
+    *pieces, spread_h, spread_l = pl.pallas_call(
         functools.partial(other_kernel, scale, cuts),
-        out_shape=[jax.ShapeDtypeStruct((n, b - a, width), F32) for a, b in zip(cuts[:-1], cuts[1:])],
-        in_specs=[SCALAR, SCALAR] + [FULL] * 4,
-        out_specs=[FULL] * (len(cuts) - 1),
-        scratch_shapes=[pltpu.VMEM((height, cols), BF16)] * 2,
+        out_shape=[jax.ShapeDtypeStruct((n, b - a, width), F32) for a, b in zip(cuts[:-1], cuts[1:])]
+        + [jax.ShapeDtypeStruct((wide, wide), BF16)] * 2,
+        in_specs=[SCALAR, SCALAR, FULL, ANY] + [FULL] * 3,
+        out_specs=[FULL] * (len(cuts) + 1),
+        scratch_shapes=[pltpu.VMEM(side.shape, F32)]
+        + [pltpu.VMEM((height, cols), BF16)] * 2
+        + [pltpu.SemaphoreType.DMA((1,))],
         compiler_params=params(24),
         cost_estimate=pl.CostEstimate(
             flops=12 * height * cols * cols, bytes_accessed=16 * height * cols, transcendentals=0
         ),
-    )(at, rows, pltpu.with_memory_space_constraint(side, pltpu.VMEM), base, lin_h, lin_l)
+    )(at, rows, table, side, base, lin_h, lin_l)
+    return pieces, (spread_h, spread_l)
 
 
 def finish_kernel(cuts, below, *refs):
-    ins, out = refs[:-1], refs[-1]
-    for i, ref in enumerate(ins):
-        rows = slice(cuts[i], cuts[i + 1])
-        out[0, :, rows] = ref[:, 0] / below[0, :, rows]
+    ins, (out, done, sems) = refs[:-3], refs[-3:]
+    copies = []
+    for c in range(done.shape[0]):
+        for i, ref in enumerate(ins):
+            rows = slice(cuts[i], cuts[i + 1])
+            done[c, :, rows] = ref[:, c] / below[c, :, rows]
+        copies.append(pltpu.make_async_copy(done.at[c], out.at[c], sems.at[c]))
+        copies[-1].start()
+    for copy in copies:
+        copy.wait()
 
 
 def finish(pieces, below, n, cuts):
     c, height, width = below.shape
     part = height // n
-    whole = pl.BlockSpec((1, n, part, width), lambda i: (i, 0, 0, 0))
     sizes = [b - a for a, b in zip(cuts[:-1], cuts[1:])]
+    shape = (c, n, part, width)
     return pl.pallas_call(
         functools.partial(finish_kernel, cuts),
-        grid=(c,),
-        out_shape=jax.ShapeDtypeStruct((c, n, part, width), F32),
-        in_specs=[whole] + [pl.BlockSpec((n, 1, rows, width), lambda i: (0, i, 0, 0)) for rows in sizes],
-        out_specs=whole,
+        out_shape=pltpu.HBM(shape, F32),
+        in_specs=[FULL] * (1 + len(pieces)),
+        out_specs=pl.BlockSpec(memory_space=pltpu.HBM),
+        scratch_shapes=[pltpu.VMEM(shape, F32), pltpu.SemaphoreType.DMA((c,))],
         compiler_params=params(12),
         cost_estimate=pl.CostEstimate(flops=c * height * width, bytes_accessed=12 * c * height * width, transcendentals=0),
-    )(below.reshape(c, n, part, width), *[p.reshape(n, c, rows, width) for p, rows in zip(pieces, sizes)]).reshape(c, height, width)
+    )(below.reshape(shape), *[p.reshape(n, c, rows, width) for p, rows in zip(pieces, sizes)]).reshape(below.shape)
 
 
 def exchange(pieces, axes):
@@ -270,8 +286,8 @@
 
     def backward(core):
         def run(at, rows, theirs, table, below, *sums):
-            cycle = other(at, rows, theirs, *sums, scale, THIRD[core])
-            back = mix((table,), exchange(cycle, CHIPS), LAST[core])
+            cycle, spread = other(at, rows, table, theirs, *sums, scale, THIRD[core])
+            back = mix(spread, exchange(cycle, CHIPS), LAST[core])
             return finish(exchange(back, "chan"), below, n_chan, LAST[core])
 
         return run

time: 148 us -> 148 us (level)
  no operation moved by 1% of the time
where the time goes in v7:
time: 148 us; the launch traced here: 147 us
  blocking collectives  125 us (84%)
  Pallas kernels  21.8 us (15%)
    all_to_all x6, blocking collectives, exchange(): lax.all_to_all(piece, axes, split_axis=0, concat_axis=0, tiled=True)  125 us
    pallas_call x1, Pallas kernels, own(): pl.pallas_call(functools.partial(own_kernel, scale, block), out_shape=[sd...  9.2 us
    pallas_call x1, Pallas kernels, other(): pl.pallas_call(functools.partial(other_kernel, scale, cuts), out_shape=[j...  5.84 us
    pallas_call x2, Pallas kernels, mix(): pl.pallas_call(functools.partial(mix_kernel, cuts, len(given)), out_shape...  3.57 us
  transfers between devices with their start and end apart: 1, of which 0 were waited for; matrix products, arithmetic and copies ran while one was open for 0% of the time, Pallas kernels for 6%

profile of v7, /device:TPU:1, one launch (start us, length us, event | category | flops | bytes accessed | tf_op | source)
XLA Modules:
  0.0 147.5 jit_solution(11381108329058243524)
XLA Ops:
  0.0 0.0 copy-start.1
  0.0 70.3 %conditional.2 = (f32[64,64,128]{2,1,0:T(8,128)S(1)}, f32[64,64]{1,0:T(8,128)S(1)}) conditional(s32[]{:T(128)} %convert_element_type.4, (f32[4,1024,128]{2,1,0:T(8,128)}, f32[64]{0:T(128)}, s32[64,64]{1,0:T(8,128)}) %tuple.19, (f32[4,1024,128]{2,1,0:T(8,128)}, f32[64]{0:T(128)}, s32[64,64]{1,0:T(8,128)}) %tuple.19), branch_computations={%region_0.0_spmd, %region_1.0_spmd} | conditional | flops 1610612736 | bytes 16777232 | solution.py:295
  0.0 1.7 %branch_0_fun.5 = (f32[16,4,16,128]{3,2,1,0:T(8,128)S(1)}, f32[16,4,48,128]{3,2,1,0:T(8,128)S(1)}, f32[64,64]{1,0:T(8,128)S(1)}, bf16[512,512]{1,0:T(8,128)(2,1)S(1)}, bf16[512,512]{1,0:T(8,128)(2,1)S(1)}) custom-call(f32[4,16,64,128]{3,2,1,0:T(8,128)} %bitcast.19, f32[64]{0:T(128)} %get-tuple-element.53.values, s32[64,64]{1,0:T(8,128)} %get-tuple-element.54.index), custom_call_target="tpu_custom_call" | custom-call | bytes 4194304 | tf_op jit(solution)/shard_map/cond/branch_0_fun/pallas_call | solution.py:84
  1.7 17.7 %all_to_all.40.refs_2_ = f32[64,16,128]{2,1,0:T(8,128)S(1)} all-to-all(f32[64,16,128]{2,1,0:T(8,128)S(1)} %bitcast.16), channel_id=1, replica_groups=mesh['chan'=16,'z'=4,'core'=2] {'chan'}, dimensions={0} | all-to-all | bytes 1048576 | tf_op jit(solution)/shard_map/cond/branch_0_fun/all_to_all | solution.py:269
  19.5 18.2 %all_to_all.41.refs_3_ = f32[64,48,128]{2,1,0:T(8,128)S(1)} all-to-all(f32[64,48,128]{2,1,0:T(8,128)S(1)} %bitcast.15), channel_id=1, replica_groups=mesh['chan'=16,'z'=4,'core'=2] {'chan'}, dimensions={0} | all-to-all | bytes 3145728 | tf_op jit(solution)/shard_map/cond/branch_0_fun/all_to_all | solution.py:269
  37.7 1.8 %branch_0_fun.6 = f32[64,64,128]{2,1,0:T(8,128)S(1)} custom-call(bf16[512,512]{1,0:T(8,128)(2,1)S(1)} %get-tuple-element.55.refs_0_, bf16[512,512]{1,0:T(8,128)(2,1)S(1)} %get-tuple-element.56.refs_1_, f32[64,16,128]{2,1,0:T(8,128)S(1)} %all_to_all.40.refs_2_, f32[64,48,128]{2,1,0:T(8,128)S(1)} %all_to_all.41.refs_3_), custom_call_target="tpu_custom_call" | custom-call | flops 1610612736 | bytes 4194304 | tf_op jit(solution)/shard_map/cond/branch_0_fun/pallas_call | solution.py:121
  39.5 30.8 %all_to_all.42 = f32[64,64,128]{2,1,0:T(8,128)S(1)} all-to-all(f32[64,64,128]{2,1,0:T(8,128)S(1)} %branch_0_fun.6), channel_id=1, replica_groups=mesh['chan'=16,'z'=4,'core'=2] {'chan','z'}, dimensions={0} | all-to-all | bytes 4194304 | tf_op jit(solution)/shard_map/cond/branch_0_fun/all_to_all | solution.py:269
  70.3 0.0 collective-permute-start
  70.3 0.0 copy-done.1
  70.3 0.0 copy-start
  70.3 9.2 %shard_map.68 = (f32[1024,512]{1,0:T(8,128)S(1)}, bf16[1024,512]{1,0:T(8,128)(2,1)S(1)}, bf16[1024,512]{1,0:T(8,128)(2,1)S(1)}) custom-call(s32[1]{0:T(128)} %bitcast.11.at, s32[4]{0:T(128)S(1)} %copy-done.1, f32[64,64,128]{2,1,0:T(8,128)S(1)} %get-tuple-element.96.side, f32[4,1024,1024]{2,1,0:T(8,128)} %inter.1), custom_call_target="tpu_custom_call" | custom-call | flops 6442450944 | bytes 10485760 | tf_op jit(solution)/shard_map/pallas_call | solution.py:170
  79.5 0.0 collective-permute-done
  79.6 0.0 copy-done
  79.6 67.7 %conditional.3 = (f32[4,1024,128]{2,1,0:T(8,128)}) conditional(s32[]{:T(128)} %convert_element_type.4, (f32[4,1024,128]{2,1,0:T(8,128)S(1)}, s32[1]{0:T(128)}, s32[4]{0:T(128)S(1)}, f32[64,64]{1,0:T(8,128)S(1)}, f32[64,64,128]{2,1,0:T(8,128)}, /*index=5*/f32[1024,512]{1,0:T(8,128)S(1)}, bf16[1024,512]{1,0:T(8,128)(2,1)S(1)}, ...), branch_computations={%region_2.0_spmd, %region_3.0_spmd} | conditional | flops 4832362496 | bytes 27262984 | solution.py:298
  79.6 5.8 %branch_0_fun.7 = (f32[64,8,128]{2,1,0:T(8,128)S(1)}, f32[64,56,128]{2,1,0:T(8,128)S(1)}, bf16[512,512]{1,0:T(8,128)(2,1)S(1)}, bf16[512,512]{1,0:T(8,128)(2,1)S(1)}) custom-call(s32[1]{0:T(128)} %get-tuple-element.68.at, s32[4]{0:T(128)S(1)} %get-tuple-element.69.rows, f32[64,64]{1,0:T(8,128)S(1)} %get-tuple-element.70.table, ...), custom_call_target="tpu_custom_call" | custom-call | flops 3221225472 | bytes 8388608 | tf_op jit(solution)/shard_map/cond/branch_0_fun/pallas_call | solution.py:222
  85.4 15.1 %all_to_all.45.refs_2_ = f32[64,8,128]{2,1,0:T(8,128)S(1)} all-to-all(f32[64,8,128]{2,1,0:T(8,128)S(1)} %get-tuple-element.77), channel_id=1, replica_groups=mesh['chan'=16,'z'=4,'core'=2] {'chan','z'}, dimensions={0} | all-to-all | bytes 524288 | tf_op jit(solution)/shard_map/cond/branch_0_fun/all_to_all | solution.py:269
  100.5 21.8 %all_to_all.46.refs_3_ = f32[64,56,128]{2,1,0:T(8,128)S(1)} all-to-all(f32[64,56,128]{2,1,0:T(8,128)S(1)} %get-tuple-element.78), channel_id=1, replica_groups=mesh['chan'=16,'z'=4,'core'=2] {'chan','z'}, dimensions={0} | all-to-all | bytes 3670016 | tf_op jit(solution)/shard_map/cond/branch_0_fun/all_to_all | solution.py:269
  122.3 1.8 %branch_0_fun.8 = f32[64,64,128]{2,1,0:T(8,128)S(1)} custom-call(bf16[512,512]{1,0:T(8,128)(2,1)S(1)} %get-tuple-element.75.refs_0_, bf16[512,512]{1,0:T(8,128)(2,1)S(1)} %get-tuple-element.76.refs_1_, f32[64,8,128]{2,1,0:T(8,128)S(1)} %all_to_all.45.refs_2_, f32[64,56,128]{2,1,0:T(8,128)S(1)} %all_to_all.46.refs_3_), custom_call_target="tpu_custom_call" | custom-call | flops 1610612736 | bytes 4194304 | tf_op jit(solution)/shard_map/cond/branch_0_fun/pallas_call | solution.py:121
  124.1 21.7 %all_to_all.47 = f32[64,64,128]{2,1,0:T(8,128)S(1)} all-to-all(f32[64,64,128]{2,1,0:T(8,128)S(1)} %branch_0_fun.8), channel_id=1, replica_groups=mesh['chan'=16,'z'=4,'core'=2] {'chan'}, dimensions={0} | all-to-all | bytes 4194304 | tf_op jit(solution)/shard_map/cond/branch_0_fun/all_to_all | solution.py:269
  145.9 1.4 branch_0_fun.9
Async XLA Ops:
  0.0 70.3 %copy-start.1 = (s32[4]{0:T(128)S(1)}, s32[4]{0:T(128)}, u32[]{:S(2)}) copy-start(s32[4]{0:T(128)} %rows.1) | copy-start | bytes 52
  70.3 9.2 %collective-permute-start = (f32[64,64,128]{2,1,0:T(8,128)S(1)}, f32[64,64,128]{2,1,0:T(8,128)}, u32[]{:S(2)}, u32[]{:S(2)}) collective-permute-start(f32[64,64,128]{2,1,0:T(8,128)S(1)} %get-tuple-element.96.side), channel_id=1, source_target_pairs={{0,1},{1,0},{2,3},{3,2},{4,5},{5,4},{6,7},{7,6},{8,9},{9,8},{10,11... | collective-permute-start | bytes 6291464 | tf_op jit(solution)/shard_map/ppermute | solution.py:296
  70.3 9.2 %copy-start = (f32[4,1024,128]{2,1,0:T(8,128)S(1)}, f32[4,1024,128]{2,1,0:T(8,128)}, u32[]{:S(2)}) copy-start(f32[4,1024,128]{2,1,0:T(8,128)} %param.15) | copy-start | bytes 6291460

commit v8 on v6

--- a/solution.py
+++ b/solution.py
@@ -8,7 +8,7 @@
 from jax.sharding import Mesh, PartitionSpec as P
 
 CHIPS = ("chan", "z")
-FIRST = ((0, 64), (0, 8, 64))
+FIRST = ((0, 64), (0, 16, 64))
 THIRD = ((0, 64), (0, 8, 64))
 LAST = ((0, 64), (0, 64))
 MIB = 2**20
@@ -142,7 +142,7 @@
             scratch_low[span, k * width : (k + 1) * width] = low
 
 
-def own_kernel(scale, block, at, rows, side, inter, acc, lin_h, lin_l, v, side_h, side_l, sem):
+def own_kernel(scale, block, at, rows, table, side, inter, acc, lin_h, lin_l, spread_h, spread_l, v, side_h, side_l, sem):
     height = v.shape[0]
     copies = [
         pltpu.make_async_copy(inter.at[at[0], pl.ds(r, block)], v.at[pl.ds(r, block)], sem.at[r // block])
@@ -151,6 +151,7 @@
     for copy in copies:
         copy.start()
     gather_side(side, rows[at[0]], side_h, side_l)
+    spread_h[...], spread_l[...] = spread_table(table[...].T)
     mine = (side_h[...], side_l[...])
     for r, copy in zip(range(0, height, block), copies):
         copy.wait()
@@ -162,16 +163,18 @@
         acc[r : r + block] += dot3(tuple(s[r : r + block] for s in mine), inner)
 
 
-def own(at, rows, side, inter, scale, block=256):
+def own(at, rows, table, side, inter, scale, block=256):
     n, part, width = side.shape
     height = inter.shape[1]
     cols = n * part * width // height
+    wide = table.shape[0] * SUB
     sds = jax.ShapeDtypeStruct
     return pl.pallas_call(
         functools.partial(own_kernel, scale, block),
-        out_shape=[sds((height, cols), F32), sds((height, cols), BF16), sds((height, cols), BF16)],
-        in_specs=[SCALAR, SCALAR, FULL, ANY],
-        out_specs=[FULL] * 3,
+        out_shape=[sds((height, cols), F32), sds((height, cols), BF16), sds((height, cols), BF16)]
+        + [sds((wide, wide), BF16)] * 2,
+        in_specs=[SCALAR, SCALAR, FULL, FULL, ANY],
+        out_specs=[FULL] * 5,
         scratch_shapes=[
             pltpu.VMEM((height, height), F32),
             pltpu.VMEM((height, cols), BF16),
@@ -185,6 +188,7 @@
     )(
         at,
         rows,
+        table,
         pltpu.with_memory_space_constraint(side, pltpu.VMEM),
         pltpu.with_memory_space_constraint(inter, pltpu.HBM),
     )
@@ -227,26 +231,32 @@
 
 
 def finish_kernel(cuts, below, *refs):
-    ins, out = refs[:-1], refs[-1]
-    for i, ref in enumerate(ins):
-        rows = slice(cuts[i], cuts[i + 1])
-        out[0, :, rows] = ref[:, 0] / below[0, :, rows]
+    ins, (out, done, sems) = refs[:-3], refs[-3:]
+    copies = []
+    for c in range(done.shape[0]):
+        for i, ref in enumerate(ins):
+            rows = slice(cuts[i], cuts[i + 1])
+            done[c, :, rows] = ref[:, c] / below[c, :, rows]
+        copies.append(pltpu.make_async_copy(done.at[c], out.at[c], sems.at[c]))
+        copies[-1].start()
+    for copy in copies:
+        copy.wait()
 
 
 def finish(pieces, below, n, cuts):
     c, height, width = below.shape
     part = height // n
-    whole = pl.BlockSpec((1, n, part, width), lambda i: (i, 0, 0, 0))
     sizes = [b - a for a, b in zip(cuts[:-1], cuts[1:])]
+    shape = (c, n, part, width)
     return pl.pallas_call(
         functools.partial(finish_kernel, cuts),
-        grid=(c,),
-        out_shape=jax.ShapeDtypeStruct((c, n, part, width), F32),
-        in_specs=[whole] + [pl.BlockSpec((n, 1, rows, width), lambda i: (0, i, 0, 0)) for rows in sizes],
-        out_specs=whole,
+        out_shape=pltpu.HBM(shape, F32),
+        in_specs=[FULL] * (1 + len(pieces)),
+        out_specs=pl.BlockSpec(memory_space=pltpu.HBM),
+        scratch_shapes=[pltpu.VMEM(shape, F32), pltpu.SemaphoreType.DMA((c,))],
         compiler_params=params(12),
         cost_estimate=pl.CostEstimate(flops=c * height * width, bytes_accessed=12 * c * height * width, transcendentals=0),
-    )(below.reshape(c, n, part, width), *[p.reshape(n, c, rows, width) for p, rows in zip(pieces, sizes)]).reshape(c, height, width)
+    )(below.reshape(shape), *[p.reshape(n, c, rows, width) for p, rows in zip(pieces, sizes)]).reshape(below.shape)
 
 
 def exchange(pieces, axes):
@@ -269,17 +279,18 @@
         return run
 
     def backward(core):
-        def run(at, rows, theirs, table, below, *sums):
+        def run(at, rows, theirs, spread, below, *sums):
             cycle = other(at, rows, theirs, *sums, scale, THIRD[core])
-            back = mix((table,), exchange(cycle, CHIPS), LAST[core])
+            back = mix(spread, exchange(cycle, CHIPS), LAST[core])
             return finish(exchange(back, "chan"), below, n_chan, LAST[core])
 
         return run
 
     mine, table = lax.cond(core == 0, forward(0), forward(1), amplitudes, sixj_values, sixj_index)
     theirs = lax.ppermute(mine, "core", [(0, 1), (1, 0)])
-    sums = own(at, ph_rows, mine, interaction, scale)
-    return lax.cond(core == 0, backward(0), backward(1), at, ph_rows, theirs, table, denominators, *sums)
+    *sums, spread_h, spread_l = own(at, ph_rows, table, mine, interaction, scale)
+    spread = (spread_h, spread_l)
+    return lax.cond(core == 0, backward(0), backward(1), at, ph_rows, theirs, spread, denominators, *sums)
 
 
 def solution(mesh):

time: 148 us -> 147 us (level)
  no operation moved by 1% of the time
where the time goes in v8:
time: 147 us
  blocking collectives  125 us (85%)
  Pallas kernels  21.3 us (14%)
    all_to_all x6, blocking collectives, exchange(): lax.all_to_all(piece, axes, split_axis=0, concat_axis=0, tiled=True)  125 us
    pallas_call x1, Pallas kernels, own(): pl.pallas_call(functools.partial(own_kernel, scale, block), out_shape=[sd...  9.19 us
    pallas_call x1, Pallas kernels, other(): pl.pallas_call(functools.partial(other_kernel, scale, cuts), out_shape=[j...  5.29 us
    pallas_call x2, Pallas kernels, mix(): pl.pallas_call(functools.partial(mix_kernel, cuts, len(given)), out_shape...  3.63 us
  transfers between devices with their start and end apart: 1, of which 0 were waited for; matrix products, arithmetic and copies ran while one was open for 0% of the time, Pallas kernels for 6%

profile of v8, /device:TPU:1, one launch (start us, length us, event | category | flops | bytes accessed | tf_op | source)
XLA Modules:
  0.0 146.9 jit_solution(17628925305768346317)
XLA Ops:
  0.0 0.0 copy-start.1
  0.0 70.3 %conditional.2 = (f32[64,64,128]{2,1,0:T(8,128)S(1)}, f32[64,64]{1,0:T(8,128)S(1)}) conditional(s32[]{:T(128)} %convert_element_type.4, (f32[4,1024,128]{2,1,0:T(8,128)}, f32[64]{0:T(128)}, s32[64,64]{1,0:T(8,128)}) %tuple.19, (f32[4,1024,128]{2,1,0:T(8,128)}, f32[64]{0:T(128)}, s32[64,64]{1,0:T(8,128)}) %tuple.19), branch_computations={%region_0.0_spmd, %region_1.0_spmd} | conditional | flops 1610612736 | bytes 16777232 | solution.py:289
  0.0 1.7 %branch_0_fun.5 = (f32[16,4,16,128]{3,2,1,0:T(8,128)S(1)}, f32[16,4,48,128]{3,2,1,0:T(8,128)S(1)}, f32[64,64]{1,0:T(8,128)S(1)}, bf16[512,512]{1,0:T(8,128)(2,1)S(1)}, bf16[512,512]{1,0:T(8,128)(2,1)S(1)}) custom-call(f32[4,16,64,128]{3,2,1,0:T(8,128)} %bitcast.19, f32[64]{0:T(128)} %get-tuple-element.57.values, s32[64,64]{1,0:T(8,128)} %get-tuple-element.58.index), custom_call_target="tpu_custom_call" | custom-call | bytes 4194304 | tf_op jit(solution)/shard_map/cond/branch_0_fun/pallas_call | solution.py:84
  1.7 17.7 %all_to_all.40.refs_2_ = f32[64,16,128]{2,1,0:T(8,128)S(1)} all-to-all(f32[64,16,128]{2,1,0:T(8,128)S(1)} %bitcast.16), channel_id=1, replica_groups=mesh['chan'=16,'z'=4,'core'=2] {'chan'}, dimensions={0} | all-to-all | bytes 1048576 | tf_op jit(solution)/shard_map/cond/branch_0_fun/all_to_all | solution.py:263
  19.5 18.2 %all_to_all.41.refs_3_ = f32[64,48,128]{2,1,0:T(8,128)S(1)} all-to-all(f32[64,48,128]{2,1,0:T(8,128)S(1)} %bitcast.15), channel_id=1, replica_groups=mesh['chan'=16,'z'=4,'core'=2] {'chan'}, dimensions={0} | all-to-all | bytes 3145728 | tf_op jit(solution)/shard_map/cond/branch_0_fun/all_to_all | solution.py:263
  37.7 1.8 %branch_0_fun.6 = f32[64,64,128]{2,1,0:T(8,128)S(1)} custom-call(bf16[512,512]{1,0:T(8,128)(2,1)S(1)} %get-tuple-element.59.refs_0_, bf16[512,512]{1,0:T(8,128)(2,1)S(1)} %get-tuple-element.60.refs_1_, f32[64,16,128]{2,1,0:T(8,128)S(1)} %all_to_all.40.refs_2_, f32[64,48,128]{2,1,0:T(8,128)S(1)} %all_to_all.41.refs_3_), custom_call_target="tpu_custom_call" | custom-call | flops 1610612736 | bytes 4194304 | tf_op jit(solution)/shard_map/cond/branch_0_fun/pallas_call | solution.py:121
  39.5 30.8 %all_to_all.42 = f32[64,64,128]{2,1,0:T(8,128)S(1)} all-to-all(f32[64,64,128]{2,1,0:T(8,128)S(1)} %branch_0_fun.6), channel_id=1, replica_groups=mesh['chan'=16,'z'=4,'core'=2] {'chan','z'}, dimensions={0} | all-to-all | bytes 4194304 | tf_op jit(solution)/shard_map/cond/branch_0_fun/all_to_all | solution.py:263
  70.3 0.0 collective-permute-start
  70.3 0.0 copy-done.1
  70.3 0.0 copy-start
  70.3 9.2 %shard_map.68 = (f32[1024,512]{1,0:T(8,128)S(1)}, bf16[1024,512]{1,0:T(8,128)(2,1)S(1)}, bf16[1024,512]{1,0:T(8,128)(2,1)S(1)}, bf16[512,512]{1,0:T(8,128)(2,1)S(1)}, bf16[512,512]{1,0:T(8,128)(2,1)S(1)}) custom-call(s32[1]{0:T(128)} %bitcast.11.at, s32[4]{0:T(128)S(1)} %copy-done.1, f32[64,64]{1,0:T(8,128)S(1)} %get-tuple-element.99.table, ...), custom_call_target="tpu_custom_call" | custom-call | flops 6442450944 | bytes 10485760 | tf_op jit(solution)/shard_map/pallas_call | solution.py:172
  79.5 0.0 collective-permute-done
  79.5 0.0 copy-done
  79.6 67.2 %conditional.3 = (f32[4,1024,128]{2,1,0:T(8,128)}) conditional(s32[]{:T(128)} %convert_element_type.4, (f32[4,1024,128]{2,1,0:T(8,128)S(1)}, s32[1]{0:T(128)}, s32[4]{0:T(128)S(1)}, f32[64,64,128]{2,1,0:T(8,128)}, f32[1024,512]{1,0:T(8,128)S(1)}, /*index=5*/bf16[1024,512]{1,0:T(8,128)(2,1)S(1)}, bf16[1024,512]{1,0:T(8,128)(2,1)S(1)}, ...), branch_computations={%region_2.0_spmd, %region_3.0_spmd} | conditional | flops 4832362496 | bytes 27262984 | solution.py:293
  79.6 5.3 %branch_0_fun.7 = (f32[64,8,128]{2,1,0:T(8,128)S(1)}, f32[64,56,128]{2,1,0:T(8,128)S(1)}) custom-call(s32[1]{0:T(128)} %get-tuple-element.74.at, s32[4]{0:T(128)S(1)} %get-tuple-element.75.rows, f32[64,64,128]{2,1,0:T(8,128)} %get-tuple-element.76.side, f32[1024,512]{1,0:T(8,128)S(1)} %get-tuple-element.77.base, ...), custom_call_target="tpu_custom_call" | custom-call | flops 3221225472 | bytes 8388608 | tf_op jit(solution)/shard_map/cond/branch_0_fun/pallas_call | solution.py:220
  84.9 15.1 %all_to_all.45.refs_2_ = f32[64,8,128]{2,1,0:T(8,128)S(1)} all-to-all(f32[64,8,128]{2,1,0:T(8,128)S(1)} %get-tuple-element.80), channel_id=1, replica_groups=mesh['chan'=16,'z'=4,'core'=2] {'chan','z'}, dimensions={0} | all-to-all | bytes 524288 | tf_op jit(solution)/shard_map/cond/branch_0_fun/all_to_all | solution.py:263
  100.0 21.8 %all_to_all.46.refs_3_ = f32[64,56,128]{2,1,0:T(8,128)S(1)} all-to-all(f32[64,56,128]{2,1,0:T(8,128)S(1)} %get-tuple-element.81), channel_id=1, replica_groups=mesh['chan'=16,'z'=4,'core'=2] {'chan','z'}, dimensions={0} | all-to-all | bytes 3670016 | tf_op jit(solution)/shard_map/cond/branch_0_fun/all_to_all | solution.py:263
  121.8 1.8 %branch_0_fun.8 = f32[64,64,128]{2,1,0:T(8,128)S(1)} custom-call(bf16[512,512]{1,0:T(8,128)(2,1)S(1)} %get-tuple-element.72.refs_0_, bf16[512,512]{1,0:T(8,128)(2,1)S(1)} %get-tuple-element.73.refs_1_, f32[64,8,128]{2,1,0:T(8,128)S(1)} %all_to_all.45.refs_2_, f32[64,56,128]{2,1,0:T(8,128)S(1)} %all_to_all.46.refs_3_), custom_call_target="tpu_custom_call" | custom-call | flops 1610612736 | bytes 4194304 | tf_op jit(solution)/shard_map/cond/branch_0_fun/pallas_call | solution.py:121
  123.7 21.7 %all_to_all.47 = f32[64,64,128]{2,1,0:T(8,128)S(1)} all-to-all(f32[64,64,128]{2,1,0:T(8,128)S(1)} %branch_0_fun.8), channel_id=1, replica_groups=mesh['chan'=16,'z'=4,'core'=2] {'chan'}, dimensions={0} | all-to-all | bytes 4194304 | tf_op jit(solution)/shard_map/cond/branch_0_fun/all_to_all | solution.py:263
  145.4 1.4 branch_0_fun.9
Async XLA Ops:
  0.0 70.3 %copy-start.1 = (s32[4]{0:T(128)S(1)}, s32[4]{0:T(128)}, u32[]{:S(2)}) copy-start(s32[4]{0:T(128)} %rows.1) | copy-start | bytes 52
  70.3 9.2 %collective-permute-start = (f32[64,64,128]{2,1,0:T(8,128)S(1)}, f32[64,64,128]{2,1,0:T(8,128)}, u32[]{:S(2)}, u32[]{:S(2)}) collective-permute-start(f32[64,64,128]{2,1,0:T(8,128)S(1)} %get-tuple-element.98.side), channel_id=1, source_target_pairs={{0,1},{1,0},{2,3},{3,2},{4,5},{5,4},{6,7},{7,6},{8,9},{9,8},{10,11... | collective-permute-start | bytes 6291464 | tf_op jit(solution)/shard_map/ppermute | solution.py:290
  70.3 9.2 %copy-start = (f32[4,1024,128]{2,1,0:T(8,128)S(1)}, f32[4,1024,128]{2,1,0:T(8,128)}, u32[]{:S(2)}) copy-start(f32[4,1024,128]{2,1,0:T(8,128)} %param.15) | copy-start | bytes 6291460
